TPU v7x, 32 devices: a whole 2x2x4 slice. The times are simulated.
32 devices in a mesh: body: 8 (over y, x, core), surf: 4 (over z).
Axes of the slice: x: 2, y: 2, z: 4, core: 2. Of those that a mesh axis runs over, the one named last changes fastest.
Arguments:
- body_panels: float32 [12, 24, 2048], P(None, 'body', 'surf'), may hold values from -6 to 48, as said below
- body_normals: float32 [3, 24, 2048], P(None, 'body', 'surf'), may hold values from -3 to 3
- fs_panels: float32 [4, 16384], P(None, ('body', 'surf')), may hold values from -6 to 48, as said below
- fs_state: float32 [2, 16384], P(None, ('body', 'surf')), may hold values from -6 to 6
- pairs: int32 [18, 2], replicated, may hold values from 0 to 23, as said below
Outputs:
- body_potential: float32 [24, 8, 2048], P('body', None, 'surf')
- body_force: float32 [24, 8, 3], P('body')
- fs_next: float32 [2, 16384], P(None, ('body', 'surf'))
Inputs may be any that keep to these rules, and one draw needn't show every extreme that they name: Rows are distinct pairs (i, j) with i < j <= i + 3, ordered by i and then by j. `body_panels`: body b's centroids lie within x in 2 b - 1 to 2 b + 1, y in -1 to 1, z in -2 to -1; areas are positive; source strengths are within -6 to 6. `fs_panels`: Free-surface panels of group g have x in 2 * 3 g - 1 to 2 * 3 (g + 1) - 1, y in -3 to 3, positive areas, source strengths within -6 to 6.
All inputs are finite; a program needn't handle non-finite values.
Results may differ from a plain program's by a relative error of at most 0.0003.
Values sent between devices are 32-bit elements; how exact they have to be, the bound alone decides.
No kernel may reach another device: no remote copies, remote signals or barrier semaphores. Data moves between devices by JAX's collectives and lax.ppermute only.
A program may use at most 64 MiB of HBM per device.

v0:
```python
import jax
import jax.numpy as jnp
from jax import lax
from jax.sharding import PartitionSpec as P

soften = 0.01
gravity = 9.81
time_step = 0.2
highest = lax.Precision.HIGHEST


def extended(block, sides, width):
    for axis, dim in sides:
        count = lax.axis_size(axis)
        forward = [(i, i + 1) for i in range(count - 1)]
        backward = [(target, source) for source, target in forward]
        low = lax.ppermute(
            lax.slice_in_dim(block, block.shape[dim] - width, None, axis=dim), axis, forward
        )
        high = lax.ppermute(lax.slice_in_dim(block, 0, width, axis=dim), axis, backward)
        block = jnp.concatenate([low, block, high], axis=dim)
    return block


def from_behind(block, axis, distance):
    devices = range(lax.axis_size(axis))
    route = [(i - distance, i) for i in devices if i - distance in devices]
    return lax.ppermute(block, axis, route)


def kernel_block(targets, sources):
    delta_x = targets[0][:, None] - sources[0][None, :]
    delta_y = targets[1][:, None] - sources[1][None, :]
    delta_z = targets[2][:, None] - sources[2][None, :]
    return lax.rsqrt(delta_x * delta_x + delta_y * delta_y + delta_z * delta_z + soften)


def surface_sweep(flat_points, flat_weights, fs_panels, step_cols):
    fs_count = fs_panels.shape[1]
    blocks = fs_count // step_cols

    def sweep_block(block_index, state_pair):
        velocity, partial_potential = state_pair
        fs_block = lax.dynamic_slice_in_dim(fs_panels, block_index * step_cols, step_cols, 1)
        delta_x = fs_block[0][None, :] - flat_points[0][:, None]
        delta_y = fs_block[1][None, :] - flat_points[1][:, None]
        delta_z = jnp.zeros_like(fs_block[0])[None, :] - flat_points[2][:, None]
        inverse = lax.rsqrt(delta_x * delta_x + delta_y * delta_y + delta_z * delta_z + soften)
        cubed = inverse * inverse * inverse
        velocity_piece = -jnp.stack(
            [
                jnp.dot(flat_weights, delta_x * cubed, precision=highest),
                jnp.dot(flat_weights, delta_y * cubed, precision=highest),
                jnp.dot(flat_weights, delta_z * cubed, precision=highest),
            ]
        )
        velocity = lax.dynamic_update_slice_in_dim(
            velocity, velocity_piece, block_index * step_cols, 1
        )
        return (velocity, partial_potential)

    start_state = (
        jnp.zeros((3, fs_count), jnp.float32),
        jnp.zeros((flat_points.shape[1],), jnp.float32),
    )
    return lax.fori_loop(0, blocks, sweep_block, start_state)


def slot_sweep(evaluate, slot_used, capacity, start_state):

    def visit_slot(slot_index, state):
        return lax.cond(
            slot_used[slot_index],
            lambda given: evaluate(given, slot_index),
            lambda given: given,
            state,
        )

    return lax.fori_loop(0, capacity, visit_slot, start_state)


def on_device(body_panels, body_normals, fs_panels, fs_state, pairs):
    bodies_dev = body_panels.shape[1]
    half_panels = body_panels.shape[2]
    panels = half_panels * lax.axis_size("surf")
    source_sets = body_panels.shape[0] - 4
    body_index = lax.axis_index("body")
    core_index = lax.axis_index("surf")
    own_full = lax.all_gather(body_panels, "surf", axis=2, tiled=True)
    first_ids = pairs[:, 0]
    second_ids = pairs[:, 1]
    first_home = first_ids // bodies_dev
    second_home = second_ids // bodies_dev
    window = extended(own_full, (("body", 1),), bodies_dev)
    window_base = (body_index - 1) * bodies_dev
    crossing = (first_home != second_home).astype(jnp.int32)
    earlier_cross = jnp.sum(
        crossing[None, :] * (first_home[None, :] < first_home[:, None]).astype(jnp.int32), axis=1
    )
    cross_rank = jnp.cumsum(crossing) - 1 - earlier_cross
    evaluator = jnp.where((crossing == 1) & (cross_rank % 2 == 1), second_home, first_home)
    capacity = bodies_dev * bodies_dev + bodies_dev * (bodies_dev + 1) // 2 // 2
    window_size = window.shape[1]
    owned = (evaluator == body_index).astype(jnp.int32)
    owned_rank = jnp.cumsum(owned) - 1
    slot_ids = jnp.arange(capacity, dtype=jnp.int32)
    slot_match = (owned[None, :] == 1) & (owned_rank[None, :] == slot_ids[:, None])
    slot_first = jnp.sum(jnp.where(slot_match, first_ids[None, :], 0), axis=1)
    slot_second = jnp.sum(jnp.where(slot_match, second_ids[None, :], 0), axis=1)
    slot_used = jnp.any(slot_match, axis=1)
    points = window[:3]
    weights = window[4:] * window[3][None]
    column_start = core_index * half_panels
    acc_half = jnp.zeros((window_size, source_sets, half_panels), jnp.float32)
    own_points_half = body_panels[:3]
    own_points = own_full[:3]
    own_weights = own_full[4:] * own_full[3][None]
    for member in range(bodies_dev):
        influence = kernel_block(own_points_half[:, member], own_points[:, member])
        self_term = lax.dot_general(
            own_weights[:, member], influence, (((1,), (1,)), ((), ())), precision=highest
        )
        acc_half = acc_half.at[bodies_dev + member].add(self_term)
    fs_half = fs_panels.shape[1]
    step_cols = min(256, fs_half)
    flat_points = own_points.reshape(3, bodies_dev * panels)
    flat_weights = own_weights[0].reshape(bodies_dev * panels)
    velocity, unused = surface_sweep(flat_points, flat_weights, fs_panels, step_cols)
    fs_whole = lax.all_gather(fs_panels, "surf", axis=1, tiled=True)
    half_points = own_points_half.reshape(3, bodies_dev * half_panels)

    def potential_block(block_index, running):
        fs_block = lax.dynamic_slice_in_dim(fs_whole, block_index * step_cols, step_cols, 1)
        surface_points = jnp.stack([fs_block[0], fs_block[1], jnp.zeros_like(fs_block[0])])
        influence = kernel_block(half_points, surface_points)
        return running + jnp.dot(influence, fs_block[2] * fs_block[3], precision=highest)

    surface_potential = lax.fori_loop(
        0,
        fs_whole.shape[1] // step_cols,
        potential_block,
        jnp.zeros((bodies_dev * half_panels,), jnp.float32),
    )
    acc_half = acc_half.at[bodies_dev : bodies_dev + bodies_dev, 0].add(
        surface_potential.reshape(bodies_dev, half_panels)
    )
    acc_full = jnp.zeros((window_size, source_sets, panels), jnp.float32)

    def evaluate_whole(state_pair, slot_index):
        half_acc, full_acc = state_pair
        near_body = slot_first[slot_index] - window_base
        far_body = slot_second[slot_index] - window_base
        targets = lax.dynamic_slice(points, (0, near_body, column_start), (3, 1, half_panels))[:, 0]
        sources = lax.dynamic_index_in_dim(points, far_body, 1, keepdims=False)
        near_weights = lax.dynamic_slice(
            weights, (0, near_body, column_start), (source_sets, 1, half_panels)
        )[:, 0]
        far_weights = lax.dynamic_index_in_dim(weights, far_body, 1, keepdims=False)
        influence = kernel_block(targets, sources)
        to_near = lax.dot_general(
            far_weights, influence, (((1,), (1,)), ((), ())), precision=highest
        )
        to_far = jnp.dot(near_weights, influence, precision=highest)
        return (half_acc.at[near_body].add(to_near), full_acc.at[far_body].add(to_far))

    acc_half, acc_full = slot_sweep(evaluate_whole, slot_used, capacity, (acc_half, acc_full))
    combined = acc_half + lax.psum_scatter(acc_full, "surf", scatter_dimension=2, tiled=True)
    upper_part = combined[bodies_dev + bodies_dev : bodies_dev + 2 * bodies_dev]
    own_potential = combined[bodies_dev : bodies_dev + bodies_dev] + from_behind(
        upper_part, "body", 1
    )
    own_potential = own_potential + from_behind(combined[:bodies_dev], "body", -1)
    area_normals = body_normals * body_panels[3][None]
    force_part = jnp.einsum("cbp,bsp->bsc", area_normals, own_potential, precision=highest)
    body_force = lax.psum(force_part, "surf")
    speed_sq = velocity[0] * velocity[0] + velocity[1] * velocity[1] + velocity[2] * velocity[2]
    next_potential = fs_state[0] + time_step * (-gravity * fs_state[1] - 0.5 * speed_sq)
    next_elevation = fs_state[1] + time_step * velocity[2]
    return (own_potential, body_force, jnp.stack([next_potential, next_elevation]))


def solution(mesh):
    placed = (
        P(None, "body", "surf"),
        P(None, "body", "surf"),
        P(None, ("body", "surf")),
        P(None, ("body", "surf")),
        P(),
    )
    return jax.shard_map(
        on_device,
        mesh=mesh,
        in_specs=placed,
        out_specs=(P("body", None, "surf"), P("body", None, None), P(None, ("body", "surf"))),
        check_vma=False,
    )
```

profile of v0, /device:TPU:5, one launch (start us, length us, event | category | flops | bytes accessed | tf_op | source)
XLA Modules:
  0.0 199.0 jit_solution(6697577241311913826)
XLA Ops:
  7.2 13.3 %all_gather.6 = f32[12,3,2048]{2,1,0:T(4,128)S(1)} all-gather(f32[12,3,512]{2,1,0:T(4,128)} %param.25), channel_id=1, replica_groups=mesh['body'=8,'surf'=4] {'surf'}, dimensions={2}, use_global_device_ids=true | all-gather | bytes 368640 | tf_op jit(solution)/shard_map/all_gather | solution.py:89
  20.5 4.3 %collective-permute-start.1 = (f32[12,3,2048]{2,1,0:T(4,128)S(1)}, f32[12,3,2048]{2,1,0:T(4,128)S(1)}, u32[]{:S(2)}, u32[]{:S(2)}) collective-permute-start(f32[12,3,2048]{2,1,0:T(4,128)S(1)} %all_gather.6), channel_id=1, source_target_pairs={{4,0},{8,4},{12,8},{16,12},{20,16},{24,20},{28,24},{5,1},{9,5},{13... | collective-permute-start | bytes 884744 | tf_op jit(solution)/shard_map/ppermute | solution.py:20
  24.8 3.0 %collective-permute-start = (f32[12,3,2048]{2,1,0:T(4,128)S(1)}, f32[12,3,2048]{2,1,0:T(4,128)S(1)}, u32[]{:S(2)}, u32[]{:S(2)}) collective-permute-start(f32[12,3,2048]{2,1,0:T(4,128)S(1)} %all_gather.6), channel_id=1, source_target_pairs={{0,4},{4,8},{8,12},{12,16},{16,20},{20,24},{24,28},{1,5},{5,9},{9,... | collective-permute-start | bytes 884744 | tf_op jit(solution)/shard_map/ppermute | solution.py:17
  27.8 0.8 compare_convert_fusion.2
  28.6 0.8 slice_bitcast_fusion.5
  29.4 0.7 slice_bitcast_fusion.3
  30.1 0.9 fusion.182
  31.0 0.7 slice_bitcast_fusion.2
  32.9 10.8 %all_gather.7 = f32[4,2048]{1,0:T(4,128)S(1)} all-gather(f32[4,512]{1,0:T(4,128)S(1)} %copy-done.2), channel_id=1, replica_groups=mesh['body'=8,'surf'=4] {'surf'}, dimensions={1}, use_global_device_ids=true | all-gather | bytes 40960 | tf_op jit(solution)/shard_map/all_gather | solution.py:129
  43.7 19.8 %while.51 = (s32[]{:T(128)}, f32[1536]{0:T(1024)S(1)}, f32[3,1536]{1,0:T(4,128)S(1)}, f32[4,2048]{1,0:T(4,128)S(1)}, f32[1536]{0:T(1024)S(1)}, /*index=5*/s32[]{...) while((s32[]{:T(128)}, f32[1536]{0:T(1024)S(1)}, f32[3,1536]{1,0:T(4,128)S(1)}, ...), condition=%wide.region_1.2_spmd.clone, body=%wide.region_0.1_spmd.clone.sunk | while | flops 7474442 | bytes 82157 | solution.py:138
  43.8 2.3 %fusion.210 = f32[1536]{0:T(1024)S(1)} fusion(f32[1536]{0:T(1024)S(1)} %get-tuple-element.768, f32[256]{0:T(256)S(1)} %bitcast.170, f32[1536]{0:T(1024)S(1)} %get-tuple-element.733, f32[256]{0:T(256)S(1)} %bitcast.169, f32[1536]{0:T(1024)S(1)} %get-tuple-element.735, f32[4,2048]{1,0:T(4,128)S(1)} %get-tuple-element.767, s32[]{:T(128)S(6)} %add.649, ...), kind=kOutput, calls=%fused_computation.91.clone.1 | convolution fusion | flops 7471360 | bytes 34828 | tf_op jit(solution)/shard_map/while/body/eval_jaxpr/dot_general | solution.py:136
  46.3 2.3 %fusion.210 = f32[1536]{0:T(1024)S(1)} fusion(f32[1536]{0:T(1024)S(1)} %get-tuple-element.768, f32[256]{0:T(256)S(1)} %bitcast.170, f32[1536]{0:T(1024)S(1)} %get-tuple-element.733, f32[256]{0:T(256)S(1)} %bitcast.169, f32[1536]{0:T(1024)S(1)} %get-tuple-element.735, f32[4,2048]{1,0:T(4,128)S(1)} %get-tuple-element.767, s32[]{:T(128)S(6)} %add.649, ...), kind=kOutput, calls=%fused_computation.91.clone.1 | convolution fusion | flops 7471360 | bytes 34828 | tf_op jit(solution)/shard_map/while/body/eval_jaxpr/dot_general | solution.py:136
  48.7 2.3 %fusion.210 = f32[1536]{0:T(1024)S(1)} fusion(f32[1536]{0:T(1024)S(1)} %get-tuple-element.768, f32[256]{0:T(256)S(1)} %bitcast.170, f32[1536]{0:T(1024)S(1)} %get-tuple-element.733, f32[256]{0:T(256)S(1)} %bitcast.169, f32[1536]{0:T(1024)S(1)} %get-tuple-element.735, f32[4,2048]{1,0:T(4,128)S(1)} %get-tuple-element.767, s32[]{:T(128)S(6)} %add.649, ...), kind=kOutput, calls=%fused_computation.91.clone.1 | convolution fusion | flops 7471360 | bytes 34828 | tf_op jit(solution)/shard_map/while/body/eval_jaxpr/dot_general | solution.py:136
  51.2 2.3 %fusion.210 = f32[1536]{0:T(1024)S(1)} fusion(f32[1536]{0:T(1024)S(1)} %get-tuple-element.768, f32[256]{0:T(256)S(1)} %bitcast.170, f32[1536]{0:T(1024)S(1)} %get-tuple-element.733, f32[256]{0:T(256)S(1)} %bitcast.169, f32[1536]{0:T(1024)S(1)} %get-tuple-element.735, f32[4,2048]{1,0:T(4,128)S(1)} %get-tuple-element.767, s32[]{:T(128)S(6)} %add.649, ...), kind=kOutput, calls=%fused_computation.91.clone.1 | convolution fusion | flops 7471360 | bytes 34828 | tf_op jit(solution)/shard_map/while/body/eval_jaxpr/dot_general | solution.py:136
  53.6 2.3 %fusion.210 = f32[1536]{0:T(1024)S(1)} fusion(f32[1536]{0:T(1024)S(1)} %get-tuple-element.768, f32[256]{0:T(256)S(1)} %bitcast.170, f32[1536]{0:T(1024)S(1)} %get-tuple-element.733, f32[256]{0:T(256)S(1)} %bitcast.169, f32[1536]{0:T(1024)S(1)} %get-tuple-element.735, f32[4,2048]{1,0:T(4,128)S(1)} %get-tuple-element.767, s32[]{:T(128)S(6)} %add.649, ...), kind=kOutput, calls=%fused_computation.91.clone.1 | convolution fusion | flops 7471360 | bytes 34828 | tf_op jit(solution)/shard_map/while/body/eval_jaxpr/dot_general | solution.py:136
  56.1 2.3 %fusion.210 = f32[1536]{0:T(1024)S(1)} fusion(f32[1536]{0:T(1024)S(1)} %get-tuple-element.768, f32[256]{0:T(256)S(1)} %bitcast.170, f32[1536]{0:T(1024)S(1)} %get-tuple-element.733, f32[256]{0:T(256)S(1)} %bitcast.169, f32[1536]{0:T(1024)S(1)} %get-tuple-element.735, f32[4,2048]{1,0:T(4,128)S(1)} %get-tuple-element.767, s32[]{:T(128)S(6)} %add.649, ...), kind=kOutput, calls=%fused_computation.91.clone.1 | convolution fusion | flops 7471360 | bytes 34828 | tf_op jit(solution)/shard_map/while/body/eval_jaxpr/dot_general | solution.py:136
  58.6 2.3 %fusion.210 = f32[1536]{0:T(1024)S(1)} fusion(f32[1536]{0:T(1024)S(1)} %get-tuple-element.768, f32[256]{0:T(256)S(1)} %bitcast.170, f32[1536]{0:T(1024)S(1)} %get-tuple-element.733, f32[256]{0:T(256)S(1)} %bitcast.169, f32[1536]{0:T(1024)S(1)} %get-tuple-element.735, f32[4,2048]{1,0:T(4,128)S(1)} %get-tuple-element.767, s32[]{:T(128)S(6)} %add.649, ...), kind=kOutput, calls=%fused_computation.91.clone.1 | convolution fusion | flops 7471360 | bytes 34828 | tf_op jit(solution)/shard_map/while/body/eval_jaxpr/dot_general | solution.py:136
  61.0 2.3 %fusion.210 = f32[1536]{0:T(1024)S(1)} fusion(f32[1536]{0:T(1024)S(1)} %get-tuple-element.768, f32[256]{0:T(256)S(1)} %bitcast.170, f32[1536]{0:T(1024)S(1)} %get-tuple-element.733, f32[256]{0:T(256)S(1)} %bitcast.169, f32[1536]{0:T(1024)S(1)} %get-tuple-element.735, f32[4,2048]{1,0:T(4,128)S(1)} %get-tuple-element.767, s32[]{:T(128)S(6)} %add.649, ...), kind=kOutput, calls=%fused_computation.91.clone.1 | convolution fusion | flops 7471360 | bytes 34828 | tf_op jit(solution)/shard_map/while/body/eval_jaxpr/dot_general | solution.py:136
  63.6 4.6 %fusion.137 = f32[1,8,512]{2,1,0:T(8,128)S(1)} fusion(f32[2048]{0:T(1024)S(1)} %bitcast.180, f32[512]{0:T(512)S(1)} %bitcast.190, f32[2048]{0:T(1024)S(1)} %bitcast.181, f32[512]{0:T(512)S(1)} %bitcast.191, f32[2048]{0:T(1024)S(1)} %bitcast.182, f32[512]{0:T(512)S(1)} %bitcast.192, f32[8,1,2048]{2,1,0:T(1,128)S(1)} %get-tuple-element.571), kind=kOutput, calls=%fused_computation.161 | convolution fusion | flops 110100480 | bytes 112640 | tf_op jit(solution)/shard_map/dot_general | solution.py:120
  68.3 4.6 %fusion.143 = f32[9,8,512]{2,1,0:T(8,128)S(1)} fusion(f32[9,8,512]{2,1,0:T(8,128)S(1)} %scatter-add.20, f32[2048]{0:T(1024)S(1)} %bitcast.177, f32[512]{0:T(512)S(1)} %bitcast.187, f32[2048]{0:T(1024)S(1)} %bitcast.178, f32[512]{0:T(512)S(1)} %bitcast.188, f32[2048]{0:T(1024)S(1)} %bitcast.179, f32[512]{0:T(512)S(1)} %bitcast.189, ...), kind=kOutput, calls=%fused_computation.163 | convolution fusion | flops 110100480 | bytes 112640 | tf_op jit(solution)/shard_map/dot_general | solution.py:120
  72.9 4.7 %fusion.152 = f32[9,8,512]{2,1,0:T(8,128)S(1)} fusion(f32[9,8,512]{2,1,0:T(8,128)S(1)} %fusion.143, f32[2048]{0:T(1024)S(1)} %bitcast.175, f32[512]{0:T(512)S(1)} %bitcast.185, f32[2048]{0:T(1024)S(1)} %bitcast.176, f32[512]{0:T(512)S(1)} %bitcast.186, f32[2048]{0:T(1024)S(1)} %bitcast.174, f32[512]{0:T(512)S(1)} %bitcast.184, ...), kind=kOutput, calls=%fused_computation.166 | convolution fusion | flops 110104576 | bytes 129024 | tf_op jit(solution)/shard_map/dot_general | solution.py:120
  77.6 0.5 scatter-add.25
  78.6 0.4 pad_maximum_fusion
  79.2 42.8 %while.49 = (s32[]{:T(128)}, f32[9,8,512]{2,1,0:T(8,128)S(1)}, f32[9,8,2048]{2,1,0:T(8,128)S(1)}, pred[12]{0:T(512)(128)(4,1)S(1)}, s32[12]{0:T(128)S(1)}, /*ind...) while((s32[]{:T(128)}, f32[9,8,512]{2,1,0:T(8,128)S(1)}, ...), condition=%wide.region_13.14_spmd, body=%wide.region_8.13_spmd.sunk | while | flops 220241968 | bytes 533004 | solution.py:79
  79.2 0.6 dynamic_slice.46
  80.5 13.7 %conditional.2 = ((f32[9,8,512]{2,1,0:T(8,128)S(1)}, f32[9,8,2048]{2,1,0:T(8,128)S(1)})) conditional(s32[]{:T(128)} %bitcast.127, (f32[9,8,512]{2,1,0:T(8,128)S(1)}, f32[9,8,2048]{2,1,0:T(8,128)S(1)}) %tuple.158, (s32[]{:T(128)}, s32[12]{0:T(128)S(1)}, s32[]{:T(128)}, f32[9,8,512]{2,1,0:T(8,128)S(1)}, s32[12]{0:T(128)S(1)}, ...), branch_computations={%region_9.9_spmd, %region_10.12_spmd} | conditional | flops 220241968 | bytes 532788 | solution.py:72
  80.5 0.6 dynamic_slice.35
  81.7 0.7 dynamic_slice.34
  83.0 1.4 and_reduce_fusion
  84.8 5.3 %fusion.23 = f32[9,8,512]{2,1,0:T(8,128)S(1)} fusion(f32[9,8,512]{2,1,0:T(8,128)S(1)} %get-tuple-element.441, s32[]{:T(128)} %select_n.100, f32[2048]{0:T(1024)S(1)} %bitcast.155, f32[512]{0:T(512)S(1)} %bitcast.161, f32[2048]{0:T(1024)S(1)} %bitcast.153, f32[512]{0:T(512)S(1)} %bitcast.159, f32[2048]{0:T(1024)S(1)} %bitcast.151, f32[512]{0:T(512)S(1)} %bitcast.157, ...), kind=kOutput, calls=%fused_computation.24 | convolution fusion | flops 110108672 | bytes 129029 | tf_op jit(solution)/shard_map/while/body/eval_jaxpr/cond/branch_1_fun/dot_general | solution.py:160
  90.0 4.1 %fusion.5 = f32[9,8,2048]{2,1,0:T(8,128)S(1)} fusion(f32[9,8,2048]{2,1,0:T(8,128)S(1)} %get-tuple-element.449, s32[]{:T(128)} %select_n.102, f32[2048]{0:T(1024)S(1)} %bitcast.156, f32[512]{0:T(512)S(1)} %bitcast.162, f32[2048]{0:T(1024)S(1)} %bitcast.154, f32[512]{0:T(512)S(1)} %bitcast.160, f32[2048]{0:T(1024)S(1)} %bitcast.152, f32[512]{0:T(512)S(1)} %bitcast.158, ...), kind=kOutput, calls=%fused_computation.6 | convolution fusion | flops 110133248 | bytes 178181 | tf_op jit(solution)/shard_map/while/body/eval_jaxpr/cond/branch_1_fun/dot_general | solution.py:163
  94.1 0.6 dynamic_slice.46
  95.4 13.7 %conditional.2 = ((f32[9,8,512]{2,1,0:T(8,128)S(1)}, f32[9,8,2048]{2,1,0:T(8,128)S(1)})) conditional(s32[]{:T(128)} %bitcast.127, (f32[9,8,512]{2,1,0:T(8,128)S(1)}, f32[9,8,2048]{2,1,0:T(8,128)S(1)}) %tuple.158, (s32[]{:T(128)}, s32[12]{0:T(128)S(1)}, s32[]{:T(128)}, f32[9,8,512]{2,1,0:T(8,128)S(1)}, s32[12]{0:T(128)S(1)}, ...), branch_computations={%region_9.9_spmd, %region_10.12_spmd} | conditional | flops 220241968 | bytes 532788 | solution.py:72
  95.4 0.6 dynamic_slice.35
  96.7 0.7 dynamic_slice.34
  98.0 1.4 and_reduce_fusion
  99.7 5.3 %fusion.23 = f32[9,8,512]{2,1,0:T(8,128)S(1)} fusion(f32[9,8,512]{2,1,0:T(8,128)S(1)} %get-tuple-element.441, s32[]{:T(128)} %select_n.100, f32[2048]{0:T(1024)S(1)} %bitcast.155, f32[512]{0:T(512)S(1)} %bitcast.161, f32[2048]{0:T(1024)S(1)} %bitcast.153, f32[512]{0:T(512)S(1)} %bitcast.159, f32[2048]{0:T(1024)S(1)} %bitcast.151, f32[512]{0:T(512)S(1)} %bitcast.157, ...), kind=kOutput, calls=%fused_computation.24 | convolution fusion | flops 110108672 | bytes 129029 | tf_op jit(solution)/shard_map/while/body/eval_jaxpr/cond/branch_1_fun/dot_general | solution.py:160
  105.0 4.1 %fusion.5 = f32[9,8,2048]{2,1,0:T(8,128)S(1)} fusion(f32[9,8,2048]{2,1,0:T(8,128)S(1)} %get-tuple-element.449, s32[]{:T(128)} %select_n.102, f32[2048]{0:T(1024)S(1)} %bitcast.156, f32[512]{0:T(512)S(1)} %bitcast.162, f32[2048]{0:T(1024)S(1)} %bitcast.154, f32[512]{0:T(512)S(1)} %bitcast.160, f32[2048]{0:T(1024)S(1)} %bitcast.152, f32[512]{0:T(512)S(1)} %bitcast.158, ...), kind=kOutput, calls=%fused_computation.6 | convolution fusion | flops 110133248 | bytes 178181 | tf_op jit(solution)/shard_map/while/body/eval_jaxpr/cond/branch_1_fun/dot_general | solution.py:163
  109.1 0.6 dynamic_slice.46
  110.4 0.6 dynamic_slice.46
  111.7 0.6 dynamic_slice.46
  113.0 0.6 dynamic_slice.46
  114.3 0.6 dynamic_slice.46
  115.6 0.6 dynamic_slice.46
  116.9 0.6 dynamic_slice.46
  118.2 0.6 dynamic_slice.46
  119.5 0.6 dynamic_slice.46
  120.7 0.6 dynamic_slice.46
  122.0 0.8 copy-done
  122.9 32.8 %while.50 = (s32[]{:T(128)}, f32[3,512]{1,0:T(4,128)S(1)}, f32[4,512]{1,0:T(4,128)S(1)}, f32[3,6144]{1,0:T(4,128)S(1)}, f32[6144]{0:T(1024)S(1)}, /*index=5*/s32[]{:T(128)}, s32[]{:T(128)}, s32[]{:T(128)}, s32[]{:T(128)}, s32[]{}) while((s32[]{:T(128)}, f32[3,512]{1,0:T(4,128)S(1)}, f32[4,512]{1,0:T(4,128)S(1)}, f32[3,6144]{1,0:T(4,128)S(1)}, ...), condition=%wide.region_17.18_spmd, body=%wide.region_16.17_spmd.sunk | while | flops 103823624 | bytes 561323 | solution.py:66
  123.2 5.4 %fusion.204 = f32[1,256]{1,0:T(1,128)S(1)} fusion(f32[6144,1]{0,1:T(1,128)S(1)} %bitcast.171, f32[6144]{0:T(1024)S(1)} %bitcast.142, f32[6144]{0:T(1024)S(1)} %mul.523, f32[6144]{0:T(1024)S(1)} %bitcast.147, f32[256]{0:T(256)S(1)} %bitcast.166, f32[6144]{0:T(1024)S(1)} %bitcast.144, f32[256]{0:T(256)S(1)} %bitcast.163), kind=kOutput, calls=%fused_computation.54.clone.1 | convolution fusion | flops 34603008 | bytes 125952 | tf_op jit(solution)/shard_map/while/body/eval_jaxpr/dot_general | solution.py:54
  128.6 5.4 %fusion.206 = f32[1,256]{1,0:T(1,128)S(1)} fusion(f32[6144,1]{0,1:T(1,128)S(1)} %bitcast.172, f32[6144]{0:T(1024)S(1)} %mul.523, f32[6144]{0:T(1024)S(1)} %bitcast.148, f32[256]{0:T(256)S(1)} %bitcast.167, f32[6144]{0:T(1024)S(1)} %bitcast.145, f32[256]{0:T(256)S(1)} %bitcast.164), kind=kOutput, calls=%fused_computation.52.clone.1 | convolution fusion | flops 34603008 | bytes 101376 | tf_op jit(solution)/shard_map/while/body/eval_jaxpr/dot_general | solution.py:52
  134.0 5.4 %fusion.205 = f32[1,256]{1,0:T(1,128)S(1)} fusion(f32[6144,1]{0,1:T(1,128)S(1)} %bitcast.173, f32[6144]{0:T(1024)S(1)} %mul.523, f32[6144]{0:T(1024)S(1)} %bitcast.149, f32[256]{0:T(256)S(1)} %bitcast.168, f32[6144]{0:T(1024)S(1)} %bitcast.146, f32[256]{0:T(256)S(1)} %bitcast.165), kind=kOutput, calls=%fused_computation.53.clone.1 | convolution fusion | flops 34603008 | bytes 101376 | tf_op jit(solution)/shard_map/while/body/eval_jaxpr/dot_general | solution.py:53
  139.6 5.4 %fusion.204 = f32[1,256]{1,0:T(1,128)S(1)} fusion(f32[6144,1]{0,1:T(1,128)S(1)} %bitcast.171, f32[6144]{0:T(1024)S(1)} %bitcast.142, f32[6144]{0:T(1024)S(1)} %mul.523, f32[6144]{0:T(1024)S(1)} %bitcast.147, f32[256]{0:T(256)S(1)} %bitcast.166, f32[6144]{0:T(1024)S(1)} %bitcast.144, f32[256]{0:T(256)S(1)} %bitcast.163), kind=kOutput, calls=%fused_computation.54.clone.1 | convolution fusion | flops 34603008 | bytes 125952 | tf_op jit(solution)/shard_map/while/body/eval_jaxpr/dot_general | solution.py:54
  144.9 5.4 %fusion.206 = f32[1,256]{1,0:T(1,128)S(1)} fusion(f32[6144,1]{0,1:T(1,128)S(1)} %bitcast.172, f32[6144]{0:T(1024)S(1)} %mul.523, f32[6144]{0:T(1024)S(1)} %bitcast.148, f32[256]{0:T(256)S(1)} %bitcast.167, f32[6144]{0:T(1024)S(1)} %bitcast.145, f32[256]{0:T(256)S(1)} %bitcast.164), kind=kOutput, calls=%fused_computation.52.clone.1 | convolution fusion | flops 34603008 | bytes 101376 | tf_op jit(solution)/shard_map/while/body/eval_jaxpr/dot_general | solution.py:52
  150.3 5.4 %fusion.205 = f32[1,256]{1,0:T(1,128)S(1)} fusion(f32[6144,1]{0,1:T(1,128)S(1)} %bitcast.173, f32[6144]{0:T(1024)S(1)} %mul.523, f32[6144]{0:T(1024)S(1)} %bitcast.149, f32[256]{0:T(256)S(1)} %bitcast.168, f32[6144]{0:T(1024)S(1)} %bitcast.146, f32[256]{0:T(256)S(1)} %bitcast.165), kind=kOutput, calls=%fused_computation.53.clone.1 | convolution fusion | flops 34603008 | bytes 101376 | tf_op jit(solution)/shard_map/while/body/eval_jaxpr/dot_general | solution.py:53
  155.8 4.4 %reduce-scatter.2.cloned.1.call-done = f32[9,8,512]{2,1,0:T(8,128)} async-done(((f32[9,8,2048]{2,1,0:T(8,128)}), f32[9,8,512]{2,1,0:T(8,128)}) %reduce-scatter.2.cloned.1.call-update) | async-done | bytes 147472 | tf_op jit(solution)/shard_map/reduce_scatter | solution.py:167
  160.1 0.9 add.328
  161.1 14.4 %collective-permute-start.2 = (f32[3,8,512]{2,1,0:T(8,128)S(1)}, f32[3,8,512]{2,1,0:T(8,128)S(1)}, u32[]{:S(2)}, u32[]{:S(2)}) collective-permute-start(f32[3,8,512]{2,1,0:T(8,128)S(1)} %get-tuple-element.572), channel_id=1, source_target_pairs={{0,4},{4,8},{8,12},{12,16},{16,20},{20,24},{24,28},{1,5},{5,9},{9,... | collective-permute-start | bytes 147464 | tf_op jit(solution)/shard_map/ppermute | solution.py:28
  175.5 1.9 collective-permute-start.3
  177.4 0.6 pad_maximum_fusion.2
  178.0 2.9 %collective-permute-done.3 = f32[3,8,512]{2,1,0:T(8,128)S(1)} collective-permute-done((f32[3,8,512]{2,1,0:T(8,128)S(1)}, f32[3,8,512]{2,1,0:T(8,128)S(1)}, u32[]{:S(2)}, u32[]{:S(2)}) %collective-permute-start.3) | collective-permute-done | bytes 49184 | tf_op jit(solution)/shard_map/ppermute | solution.py:28
  180.9 0.2 fusion.162
  181.1 10.9 %psum.7 = f32[3,8,3]{1,2,0:T(4,128)} all-reduce(f32[3,8,3]{1,2,0:T(4,128)S(1)} %fusion.162), channel_id=1, replica_groups=mesh['body'=8,'surf'=4] {'surf'}, use_global_device_ids=true, to_apply=%region_15.16 | all-reduce | flops 72 | bytes 576 | tf_op jit(solution)/shard_map/psum | solution.py:175
  (101 shorter events, 4.0 us)
Async XLA Ops:
  7.2 25.7 %copy-start.2 = (f32[4,512]{1,0:T(4,128)S(1)}, f32[4,512]{1,0:T(4,128)}, u32[]{:S(2)}) copy-start(f32[4,512]{1,0:T(4,128)} %param.27) | copy-start | bytes 24580
  7.2 153.0 %reduce-scatter.2.cloned.1.call-start = ((), (), s32[]{:S(2)}) async-start(), calls=%async_computation.1 | async-start | bytes 737280 | tf_op jit(solution)/shard_map/reduce_scatter | solution.py:167
  20.5 58.0 %collective-permute-start.1 = (f32[12,3,2048]{2,1,0:T(4,128)S(1)}, f32[12,3,2048]{2,1,0:T(4,128)S(1)}, u32[]{:S(2)}, u32[]{:S(2)}) collective-permute-start(f32[12,3,2048]{2,1,0:T(4,128)S(1)} %all_gather.6), channel_id=1, source_target_pairs={{4,0},{8,4},{12,8},{16,12},{20,16},{24,20},{28,24},{5,1},{9,5},{13... | collective-permute-start | bytes 884744 | tf_op jit(solution)/shard_map/ppermute | solution.py:20
  24.8 53.7 %collective-permute-start = (f32[12,3,2048]{2,1,0:T(4,128)S(1)}, f32[12,3,2048]{2,1,0:T(4,128)S(1)}, u32[]{:S(2)}, u32[]{:S(2)}) collective-permute-start(f32[12,3,2048]{2,1,0:T(4,128)S(1)} %all_gather.6), channel_id=1, source_target_pairs={{0,4},{4,8},{8,12},{12,16},{16,20},{20,24},{24,28},{1,5},{5,9},{9,... | collective-permute-start | bytes 884744 | tf_op jit(solution)/shard_map/ppermute | solution.py:17
  122.0 0.8 copy-start
  122.9 32.8 %copy-start.4 = (f32[2,512]{1,0:T(2,128)S(1)}, f32[2,512]{1,0:T(2,128)}, u32[]{:S(2)}) copy-start(f32[2,512]{1,0:T(2,128)} %param.28) | copy-start | bytes 12292
  122.9 32.9 %copy-start.3 = (f32[3,3,512]{2,1,0:T(4,128)S(1)}, f32[3,3,512]{2,1,0:T(4,128)}, u32[]{:S(2)}) copy-start(f32[3,3,512]{2,1,0:T(4,128)} %param.26) | copy-start | bytes 55300
  161.1 16.9 %collective-permute-start.2 = (f32[3,8,512]{2,1,0:T(8,128)S(1)}, f32[3,8,512]{2,1,0:T(8,128)S(1)}, u32[]{:S(2)}, u32[]{:S(2)}) collective-permute-start(f32[3,8,512]{2,1,0:T(8,128)S(1)} %get-tuple-element.572), channel_id=1, source_target_pairs={{0,4},{4,8},{8,12},{12,16},{16,20},{20,24},{24,28},{1,5},{5,9},{9,... | collective-permute-start | bytes 147464 | tf_op jit(solution)/shard_map/ppermute | solution.py:28
  175.5 5.4 %collective-permute-start.3 = (f32[3,8,512]{2,1,0:T(8,128)S(1)}, f32[3,8,512]{2,1,0:T(8,128)S(1)}, u32[]{:S(2)}, u32[]{:S(2)}) collective-permute-start(f32[3,8,512]{2,1,0:T(8,128)S(1)} %get-tuple-element.573), channel_id=1, source_target_pairs={{4,0},{8,4},{12,8},{16,12},{20,16},{24,20},{28,24},{5,1},{9,5},{13... | collective-permute-start | bytes 147464 | tf_op jit(solution)/shard_map/ppermute | solution.py:28
  180.9 11.1 %copy-start.1 = (f32[3,8,512]{2,1,0:T(8,128)}, f32[3,8,512]{2,1,0:T(8,128)S(1)}, u32[]{:S(2)}) copy-start(f32[3,8,512]{2,1,0:T(8,128)S(1)} %fusion.161) | copy-start | bytes 147460
Sparse Core Ops, SparseCore 0:
  123.0 37.0 reduce-scatter.1
where the time goes:
time: 203 us; the launch traced here: 199 us
  matrix products  83.5 us (41%)
  blocking collectives  35 us (17%)
  starting transfers between devices  23.6 us (12%)
  local copies, waits for them, and re-layouts  15.9 us (8%)
  between operations  14.6 us (7%)
  loops' own time  11.5 us (6%)
  other arithmetic  7.72 us (4%)
  waiting for transfers between devices  7.26 us (4%)
    dot_general x8, matrix products, potential_block(): jnp.dot(influence, fs_block[2] * fs_block[3], precision=highest)  18.3 us
    ppermute x2, starting transfers between devices, from_behind(): return lax.ppermute(block, axis, route)  16.3 us
    dot_general x3, matrix products, on_device(): lax.dot_general(own_weights[:, member], influence, (((1,), (1,)), ((), ()...  13.9 us
    all_gather x1, blocking collectives, on_device(): own_full = lax.all_gather(body_panels, 'surf', axis=2, tiled=True)  13.3 us
    psum x1, blocking collectives, on_device(): body_force = lax.psum(force_part, 'surf')  10.9 us
    all_gather x1, blocking collectives, on_device(): fs_whole = lax.all_gather(fs_panels, 'surf', axis=1, tiled=True)  10.8 us
    dot_general x2, matrix products, sweep_block(): jnp.dot(flat_weights, delta_z * cubed, precision=highest)  10.8 us
    dot_general x2, matrix products, sweep_block(): jnp.dot(flat_weights, delta_y * cubed, precision=highest)  10.7 us
  transfers between devices with their start and end apart: 5, of which 2 were waited for; matrix products, arithmetic and copies ran while one was open for 36% of the time, Pallas kernels for 0%

commit v1 on v0

v1 whole, which is shorter than its diff:
```python
import functools

import jax
import jax.numpy as jnp
from jax import lax
from jax.experimental import pallas as pl
from jax.experimental.pallas import tpu as pltpu
from jax.sharding import PartitionSpec as P

soften = 0.01
gravity = 9.81
time_step = 0.2
mid_depth = -1.5
half = jnp.bfloat16
full = jnp.float32
DEPTH = 48


def rows_of(block_shape, rows):
    index = lax.broadcasted_iota(jnp.int32, block_shape, 0)
    block = jnp.zeros(block_shape, full)
    for position, row in enumerate(rows):
        block = jnp.where(index == position, row, block)
    return block


def three_parts(block):
    first = block.astype(half).astype(full)
    rest = block - first
    second = rest.astype(half).astype(full)
    return first, second, rest - second


def source_features(x, y, z):
    norm = x * x + y * y + z * z
    a, b, c = three_parts(rows_of((8, x.shape[1]), (x, y, z, norm, 1.0)))
    return jnp.concatenate([a, b, a, b, c, a], axis=0).T.astype(half)


def target_features(x, y, z):
    norm = x * x + y * y + z * z + soften
    a, b, c = three_parts(rows_of((8, x.shape[1]), (-2.0 * x, -2.0 * y, -2.0 * z, 1.0, norm)))
    return jnp.concatenate([a, a, b, b, a, c], axis=0).astype(half)


def two_parts(block):
    first = block.astype(half)
    return first, (block - first.astype(full)).astype(half)


def split_weights(block):
    first = block.astype(half).astype(full)
    return jnp.concatenate([first, block - first], axis=0).astype(half)


def product(left, right):
    return jnp.dot(left, right, preferred_element_type=full)


def weighted_sum(values, weights):
    high, low = two_parts(values)
    both = product(
        jnp.concatenate([weights, weights], axis=1), jnp.concatenate([high, low], axis=0)
    )
    return both[:8] + both[8:]


def influence_sum(targets, sources, weights):
    return weighted_sum(lax.rsqrt(product(sources, targets)), weights)


def point_row(bodies, member, axis):
    return 8 * bodies + 3 * member + axis


def surface_row(bodies, entry):
    return 11 * bodies + entry


def tile_rows(bodies):
    return -(-(11 * bodies + 3) // 8) * 8


def body_points(tile, bodies, member):
    return [
        tile[point_row(bodies, member, axis) : point_row(bodies, member, axis) + 1, :]
        for axis in range(3)
    ]


def surface_points(tile, bodies):
    x, y, weight = [
        tile[surface_row(bodies, entry) : surface_row(bodies, entry) + 1, :] for entry in range(3)
    ]
    return x, y, jnp.full_like(x, -mid_depth), weight


def pack_kernel(base_ref, panels_ref, surface_ref, tile_ref):
    bodies = panels_ref.shape[1]
    base = base_ref[0]
    tile_ref[...] = jnp.zeros_like(tile_ref)
    area = panels_ref[3]
    for member in range(bodies):
        for entry in range(8):
            tile_ref[8 * member + entry : 8 * member + entry + 1, :] = (
                panels_ref[4 + entry, member : member + 1, :] * area[member : member + 1, :]
            )
        centre = (2 * (base + member)).astype(full)
        for axis, shift in enumerate((centre, 0.0, mid_depth)):
            row = point_row(bodies, member, axis)
            tile_ref[row : row + 1, :] = panels_ref[axis, member : member + 1, :] - shift
    group_centre = (2 * base + (bodies - 1)).astype(full)
    row = surface_row(bodies, 0)
    tile_ref[row : row + 1, :] = surface_ref[0:1, :] - group_centre
    tile_ref[row + 1 : row + 2, :] = surface_ref[1:2, :]
    tile_ref[row + 2 : row + 3, :] = surface_ref[2:3, :] * surface_ref[3:4, :]


def prepare_bodies(tile, bodies, columns, features, weights, offset=0):
    for member in range(bodies):
        features[offset + member, columns, :] = source_features(*body_points(tile, bodies, member))
        weights[offset + member, :, columns] = split_weights(tile[8 * member : 8 * member + 8, :])


def prepare_surface(tile, bodies, columns, features, weights, slot):
    x, y, z, weight = surface_points(tile, bodies)
    features[slot, columns, :] = source_features(x, y, z)
    weights[slot, :, columns] = split_weights(rows_of((8, x.shape[1]), (weight,)))


def own_tile_kernel(bodies, tile_ref, acc_ref, features, weights):
    width = tile_ref.shape[1]
    tile = tile_ref[...]
    columns = pl.ds(0, width)
    prepare_bodies(tile, bodies, columns, features, weights)
    prepare_surface(tile, bodies, columns, features, weights, bodies)
    for member in range(bodies):
        x, y, z = body_points(tile, bodies, member)
        self_part = influence_sum(target_features(x, y, z), features[member], weights[member])
        shift = float(2 * member - bodies + 1)
        surface_part = influence_sum(
            target_features(x + shift, y, z), features[bodies], weights[bodies]
        )
        acc_ref[member] = self_part + surface_part


def group_kernel(bodies, base_ref, pairs_ref, tiles_ref, given_ref, acc_ref, features, weights, points):
    count, _, width = tiles_ref.shape
    base = base_ref[0]
    for index in range(count):
        tile = tiles_ref[index]
        columns = pl.ds(index * width, width)
        prepare_bodies(tile, bodies, columns, features, weights)
        prepare_surface(tile, bodies, columns, features, weights, bodies)
    own = tiles_ref[0]
    for member in range(bodies):
        points[member] = rows_of((8, width), body_points(own, bodies, member))
    acc_ref[...] = given_ref[...]

    def targets_of(member, shift):
        block = points[member]
        return target_features(block[0:1] + shift, block[1:2], block[2:3])

    def own_step(step, carry):
        member = step // 2
        on_surface = step % 2
        source = jnp.where(on_surface == 1, bodies, member)
        shift = jnp.where(on_surface == 1, 2 * member - bodies + 1, 0).astype(full)
        acc_ref[member] += influence_sum(
            targets_of(member, shift), features[source, width:, :], weights[source, :, width:]
        )
        return carry

    lax.fori_loop(0, 2 * bodies, own_step, 0)

    def pair_step(step, carry):
        target = pairs_ref[step // 2, step % 2] - base
        source = pairs_ref[step // 2, 1 - step % 2] - base
        inside = (target >= 0) & (target < bodies) & (source >= 0) & (source < bodies)

        @pl.when(inside)
        def _():
            shift = (2 * (target - source)).astype(full)
            acc_ref[target] += influence_sum(
                targets_of(target, shift), features[source], weights[source]
            )

        return carry

    lax.fori_loop(0, 2 * pairs_ref.shape[0], pair_step, 0)


def crossing_kernel(
    bodies, base_ref, pairs_ref, lower_ref, upper_ref, tile_ref, panels_ref, normals_ref, given_ref,
    acc_ref, force_ref, features, weights, points,
):
    count, _, width = lower_ref.shape
    base = base_ref[0]
    for index in range(count):
        columns = pl.ds(index * width, width)
        prepare_bodies(lower_ref[index], bodies, columns, features, weights)
        prepare_bodies(upper_ref[index], bodies, columns, features, weights, bodies)
    own = tile_ref[...]
    for member in range(bodies):
        points[member] = rows_of((8, width), body_points(own, bodies, member))
    acc_ref[...] = given_ref[...]

    def pair_step(step, carry):
        target = pairs_ref[step // 2, step % 2] - base
        source = pairs_ref[step // 2, 1 - step % 2] - base
        crossing = (target >= 0) & (target < bodies) & ((source < 0) | (source >= bodies))

        @pl.when(crossing)
        def _():
            shift = (2 * (target - source)).astype(full)
            slot = jnp.where(source < 0, source + bodies, source)
            block = points[target]
            acc_ref[target] += influence_sum(
                target_features(block[0:1] + shift, block[1:2], block[2:3]),
                features[slot],
                weights[slot],
            )

        return carry

    lax.fori_loop(0, 2 * pairs_ref.shape[0], pair_step, 0)
    lane = lax.broadcasted_iota(jnp.int32, (8, 128), 1)
    for member in range(bodies):
        potential = acc_ref[member]
        area = panels_ref[3, member : member + 1, :]
        out = jnp.zeros((8, 128), full)
        for axis in range(3):
            term = potential * (normals_ref[axis, member : member + 1, :] * area)
            out = jnp.where(lane == axis, jnp.sum(term, axis=1, keepdims=True), out)
        force_ref[member] = out


def velocity_kernel(bodies, tiles_ref, state_ref, next_ref, features, weights):
    count, _, width = tiles_ref.shape
    for index in range(count):
        tile = tiles_ref[index]
        columns = pl.ds(index * width, width)
        for member in range(bodies):
            x, y, z = body_points(tile, bodies, member)
            features[member, columns, :] = source_features(x, y, z)
            first = tile[8 * member : 8 * member + 1, :]
            weights[member, :, columns] = split_weights(
                rows_of((8, width), (first, first * x, first * y, first * z))
            )
    own = tiles_ref[0]
    x, y, z, _ = surface_points(own, bodies)

    def body_step(member, velocity):
        place = x + (bodies - 1 - 2 * member).astype(full)
        inverse = lax.rsqrt(product(features[member], target_features(place, y, z)))
        moments = weighted_sum(inverse * inverse * inverse, weights[member])
        return tuple(
            so_far + (moments[axis + 1 : axis + 2] - at * moments[0:1])
            for axis, (so_far, at) in enumerate(zip(velocity, (place, y, z)))
        )

    zero = jnp.zeros((1, width), full)
    velocity = lax.fori_loop(0, bodies, body_step, (zero, zero, zero))
    speed_sq = velocity[0] * velocity[0] + velocity[1] * velocity[1] + velocity[2] * velocity[2]
    potential, elevation = state_ref[0:1, :], state_ref[1:2, :]
    next_ref[0:1, :] = potential + time_step * (-gravity * elevation - 0.5 * speed_sq)
    next_ref[1:2, :] = elevation + time_step * velocity[2]


def call(kernel, out_shapes, operands, scalars=0, scratch=(), units=0.0):
    specs = [pl.BlockSpec(memory_space=pltpu.SMEM)] * scalars
    specs += [pl.BlockSpec(memory_space=pltpu.VMEM)] * (len(operands) - scalars)
    several = isinstance(out_shapes, list)
    shapes = [jax.ShapeDtypeStruct(shape, full) for shape in (out_shapes if several else [out_shapes])]
    result = pl.pallas_call(
        kernel,
        out_shape=shapes,
        in_specs=specs,
        out_specs=[pl.BlockSpec(memory_space=pltpu.VMEM)] * len(shapes),
        scratch_shapes=list(scratch),
        compiler_params=pltpu.CompilerParams(vmem_limit_bytes=48 * 1024 * 1024),
        cost_estimate=pl.CostEstimate(
            flops=int(units * 1.2e9), bytes_accessed=1024, transcendentals=0
        ),
    )(*operands)
    return result if several else result[0]


def rotations(block, axis):
    count = lax.axis_size(axis)
    return [
        lax.ppermute(block, axis, [(i, (i + k) % count) for i in range(count)])
        for k in range(1, count)
    ]


def on_device(body_panels, body_normals, fs_panels, fs_state, pairs):
    bodies = body_panels.shape[1]
    width = body_panels.shape[2]
    tiles_count = lax.axis_size("surf")
    groups = lax.axis_size("body")
    base = (lax.axis_index("body") * bodies).astype(jnp.int32).reshape(1)
    own = call(
        pack_kernel, (tile_rows(bodies), width), (base, body_panels, fs_panels), scalars=1
    )
    if tiles_count == 4:
        tiles = jnp.stack([own] + rotations(own, "surf"))
    else:
        everything = lax.all_gather(own, "surf")
        tiles = jnp.concatenate(
            [own[None]]
            + [
                lax.dynamic_index_in_dim(
                    everything, (lax.axis_index("surf") + k) % tiles_count, 0
                )
                for k in range(1, tiles_count)
            ]
        )
    wide = width * tiles_count
    acc_shape = (bodies, 8, width)
    partial = call(
        functools.partial(own_tile_kernel, bodies),
        acc_shape,
        (own,),
        scratch=(
            pltpu.VMEM((bodies + 1, width, DEPTH), half),
            pltpu.VMEM((bodies + 1, 16, width), half),
        ),
        units=2.0,
    )
    lower = lax.ppermute(tiles, "body", [(i, i + 1) for i in range(groups - 1)])
    upper = lax.ppermute(tiles, "body", [(i + 1, i) for i in range(groups - 1)])
    points = pltpu.VMEM((bodies, 8, width), full)
    partial = call(
        functools.partial(group_kernel, bodies),
        acc_shape,
        (base, pairs, tiles, partial),
        scalars=2,
        scratch=(
            pltpu.VMEM((bodies + 1, wide, DEPTH), half),
            pltpu.VMEM((bodies + 1, 16, wide), half),
            points,
        ),
        units=7.0,
    )
    own_potential, force = call(
        functools.partial(crossing_kernel, bodies),
        [acc_shape, (bodies, 8, 128)],
        (base, pairs, lower, upper, own, body_panels, body_normals, partial),
        scalars=2,
        scratch=(
            pltpu.VMEM((2 * bodies, wide, DEPTH), half),
            pltpu.VMEM((2 * bodies, 16, wide), half),
            points,
        ),
        units=6.0,
    )
    fs_next = call(
        functools.partial(velocity_kernel, bodies),
        (2, width),
        (tiles, fs_state),
        scratch=(
            pltpu.VMEM((bodies, wide, DEPTH), half),
            pltpu.VMEM((bodies, 16, wide), half),
        ),
        units=5.0,
    )
    if tiles_count == 4:
        first, second, third = rotations(force, "surf")
        total = (force + second) + (first + third)
    else:
        total = lax.psum(force, "surf")
    return own_potential, total[:, :, :3], fs_next


def solution(mesh):
    placed = (
        P(None, "body", "surf"),
        P(None, "body", "surf"),
        P(None, ("body", "surf")),
        P(None, ("body", "surf")),
        P(),
    )
    return jax.shard_map(
        on_device,
        mesh=mesh,
        in_specs=placed,
        out_specs=(P("body", None, "surf"), P("body", None, None), P(None, ("body", "surf"))),
        check_vma=False,
    )
```

time: 203 us -> 49.4 us (0.24)
  the two profiles are of different devices: /device:TPU:5 before, /device:TPU:1 now
where the time goes in v1:
time: 49.4 us; the launch traced here: 48.5 us
  Pallas kernels  26.7 us (54%)
  starting transfers between devices  13.8 us (28%)
  waiting for transfers between devices  4.82 us (10%)
  local copies, waits for them, and re-layouts  2.38 us (5%)
  between operations  0.76 us (2%)
    pallas_call x5, Pallas kernels, call(): pl.pallas_call(kernel, out_shape=shapes, in_specs=specs, out_specs=[pl.Bl...  26.7 us
    ppermute x6, starting transfers between devices, rotations(): lax.ppermute(block, axis, [(i, (i + k) % count) for i in range(count)])  7.95 us
    ppermute x6, waiting for transfers between devices, rotations(): lax.ppermute(block, axis, [(i, (i + k) % count) for i in range(count)])  4.81 us
    ppermute x1, starting transfers between devices, on_device(): lower = lax.ppermute(tiles, 'body', [(i, i + 1) for i in range(groups - 1)])  3.02 us
    ppermute x1, starting transfers between devices, on_device(): upper = lax.ppermute(tiles, 'body', [(i + 1, i) for i in range(groups - 1)])  2.85 us
    unnamed x14, local copies, waits for them, and re-layouts  2.38 us
  transfers between devices with their start and end apart: 8, of which 1 were waited for; matrix products, arithmetic and copies ran while one was open for 0% of the time, Pallas kernels for 42%

profile of v1, /device:TPU:1, one launch (start us, length us, event | category | flops | bytes accessed | tf_op | source)
XLA Modules:
  0.0 48.5 jit_solution(18083160689014055994)
XLA Ops:
  0.6 0.0 copy-start.2
  0.6 0.7 %copy-done.2 = f32[4,512]{1,0:T(4,128)S(1)} copy-done((f32[4,512]{1,0:T(4,128)S(1)}, f32[4,512]{1,0:T(4,128)}, u32[]{:S(2)}) %copy-start.2) | copy-done | bytes 8216
  1.3 0.0 copy-start
  1.3 0.9 %copy-done = f32[12,3,512]{2,1,0:T(4,128)S(1)} copy-done((f32[12,3,512]{2,1,0:T(4,128)S(1)}, f32[12,3,512]{2,1,0:T(4,128)}, u32[]{:S(2)}) %copy-start) | copy-done | bytes 73752
  2.2 0.0 copy-start.5
  2.3 4.2 %collective-permute-start.2 = (f32[40,512]{1,0:T(8,128)S(1)}, f32[40,512]{1,0:T(8,128)S(1)}, u32[]{:S(2)}, u32[]{:S(2)}) collective-permute-start(f32[40,512]{1,0:T(8,128)S(1)} %shard_map.76.tile_ref), channel_id=1, source_target_pairs={{0,3},{1,0},{2,1},{3,2},{4,7},{5,4},{6,5},{7,6},{8,11},{9,8},{10,9... | collective-permute-start | bytes 245768 | tf_op jit(solution)/shard_map/ppermute | solution.py:292
  6.5 0.0 collective-permute-start.1
  6.5 0.5 collective-permute-start
  6.9 2.3 %shard_map.77.given_ref = f32[3,8,512]{2,1,0:T(8,128)S(1)} custom-call(f32[40,512]{1,0:T(8,128)S(1)} %shard_map.76.tile_ref), custom_call_target="tpu_custom_call" | custom-call | flops 2400000000 | bytes 1024 | tf_op jit(solution)/shard_map/pallas_call | solution.py:275
  9.2 0.0 copy-done.5
  9.2 0.1 copy.9.pairs_ref
  9.3 0.0 collective-permute-done.2
  9.3 4.8 %collective-permute-done.1 = f32[40,512]{1,0:T(8,128)S(1)} collective-permute-done((f32[40,512]{1,0:T(8,128)S(1)}, f32[40,512]{1,0:T(8,128)S(1)}, u32[]{:S(2)}, u32[]{:S(2)}) %collective-permute-start.1) | collective-permute-done | bytes 81952 | tf_op jit(solution)/shard_map/ppermute | solution.py:292
  14.1 0.0 collective-permute-done
  14.2 0.0 copy-start.1
  14.2 0.0 copy-start.3
  14.2 2.8 %collective-permute-start.4 = (f32[4,40,512]{2,1,0:T(8,128)S(1)}, f32[4,40,512]{2,1,0:T(8,128)S(1)}, u32[]{:S(2)}, u32[]{:S(2)}) collective-permute-start(f32[4,40,512]{2,1,0:T(8,128)S(1)} %pad_maximum_fusion.tiles_ref), channel_id=1, source_target_pairs={{4,0},{8,4},{12,8},{16,12},{20,16},{24,20},{28,24},{5,1},{9,5},{13... | collective-permute-start | bytes 983048 | tf_op jit(solution)/shard_map/ppermute | solution.py:332
  17.0 3.0 %collective-permute-start.3 = (f32[4,40,512]{2,1,0:T(8,128)S(1)}, f32[4,40,512]{2,1,0:T(8,128)S(1)}, u32[]{:S(2)}, u32[]{:S(2)}) collective-permute-start(f32[4,40,512]{2,1,0:T(8,128)S(1)} %pad_maximum_fusion.tiles_ref), channel_id=1, source_target_pairs={{0,4},{4,8},{8,12},{12,16},{16,20},{20,24},{24,28},{1,5},{5,9},{9,... | collective-permute-start | bytes 983048 | tf_op jit(solution)/shard_map/ppermute | solution.py:331
  20.1 12.4 %shard_map.78.given_ref = f32[3,8,512]{2,1,0:T(8,128)S(1)} custom-call(s32[1]{0:T(128)} %bitcast.base_ref, s32[18,2]{1,0:T(8,128)S(1)} %copy.9.pairs_ref, f32[4,40,512]{2,1,0:T(8,128)S(1)} %pad_maximum_fusion.tiles_ref, f32[3,8,512]{2,1,0:T(8,128)S(1)} %shard_map.77.given_ref), custom_call_target="tpu_custom_call" | custom-call | flops 8400000000 | bytes 1024 | tf_op jit(solution)/shard_map/pallas_call | solution.py:275
  32.4 0.0 copy-start.4
  32.4 0.0 collective-permute-done.4.upper_ref
  32.5 0.0 collective-permute-done.3.lower_ref
  32.5 0.0 copy-done.1
  32.5 0.0 copy-done.3
  32.5 6.5 %shard_map.79 = (f32[3,8,512]{2,1,0:T(8,128)}, f32[3,8,128]{2,1,0:T(8,128)S(1)}) custom-call(s32[1]{0:T(128)} %bitcast.base_ref, s32[18,2]{1,0:T(8,128)S(1)} %copy.9.pairs_ref, f32[4,40,512]{2,1,0:T(8,128)S(1)} %collective-permute-done.3.lower_ref, f32[4,40,512]{2,1,0:T(8,128)S(1)} %collective-permute-done.4.upper_ref, f32[40,512]{1,0:T(8,128)S(1)} %shard_map.76.tile_ref, ...), custom_call_target="tpu_custom_call" | custom-call | flops 7200000000 | bytes 1024 | tf_op jit(solution)/shard_map/pallas_call | solution.py:275
  39.0 1.8 %collective-permute-start.7 = (f32[3,8,128]{2,1,0:T(8,128)S(1)}, f32[3,8,128]{2,1,0:T(8,128)S(1)}, u32[]{:S(2)}, u32[]{:S(2)}) collective-permute-start(f32[3,8,128]{2,1,0:T(8,128)S(1)} %get-tuple-element.6), channel_id=1, source_target_pairs={{0,3},{1,0},{2,1},{3,2},{4,7},{5,4},{6,5},{7,6},{8,11},{9,8},{10,9... | collective-permute-start | bytes 36872 | tf_op jit(solution)/shard_map/ppermute | solution.py:292
  40.8 0.0 collective-permute-start.6
  40.8 1.4 %collective-permute-start.5 = (f32[3,8,128]{2,1,0:T(8,128)S(1)}, f32[3,8,128]{2,1,0:T(8,128)S(1)}, u32[]{:S(2)}, u32[]{:S(2)}) collective-permute-start(f32[3,8,128]{2,1,0:T(8,128)S(1)} %get-tuple-element.6), channel_id=1, source_target_pairs={{0,2},{1,3},{2,0},{3,1},{4,6},{5,7},{6,4},{7,5},{8,10},{9,11},{10,... | collective-permute-start | bytes 36872 | tf_op jit(solution)/shard_map/ppermute | solution.py:292
  42.3 0.0 copy-done.4
  42.3 5.5 %shard_map.80 = f32[2,512]{1,0:T(2,128)} custom-call(f32[4,40,512]{2,1,0:T(8,128)S(1)} %pad_maximum_fusion.tiles_ref, f32[2,512]{1,0:T(2,128)S(1)} %copy-done.4), custom_call_target="tpu_custom_call" | custom-call | flops 6000000000 | bytes 1024 | tf_op jit(solution)/shard_map/pallas_call | solution.py:275
  47.8 0.0 collective-permute-done.7
  47.8 0.0 collective-permute-done.6
  47.8 0.0 collective-permute-done.5
  47.8 0.7 %copy.10 = f32[3,8,3]{1,2,0:T(4,128)} copy(f32[3,8,3]{2,1,0:T(8,128)S(1)} %fusion) | data formatting | bytes 576
  (3 shorter events, 0.1 us)
Async XLA Ops:
  0.6 0.7 %copy-start.2 = (f32[4,512]{1,0:T(4,128)S(1)}, f32[4,512]{1,0:T(4,128)}, u32[]{:S(2)}) copy-start(f32[4,512]{1,0:T(4,128)} %surface_ref.1) | copy-start | bytes 24580
  1.3 0.9 %copy-start = (f32[12,3,512]{2,1,0:T(4,128)S(1)}, f32[12,3,512]{2,1,0:T(4,128)}, u32[]{:S(2)}) copy-start(f32[12,3,512]{2,1,0:T(4,128)} %panels_ref.3) | copy-start | bytes 221188
  2.2 7.0 %copy-start.5 = (s32[18,2]{0,1:T(2,128)S(1)}, s32[18,2]{0,1:T(2,128)}, u32[]{:S(2)}) copy-start(s32[18,2]{0,1:T(2,128)} %param.9) | copy-start | bytes 436
  2.3 7.1 %collective-permute-start.2 = (f32[40,512]{1,0:T(8,128)S(1)}, f32[40,512]{1,0:T(8,128)S(1)}, u32[]{:S(2)}, u32[]{:S(2)}) collective-permute-start(f32[40,512]{1,0:T(8,128)S(1)} %shard_map.76.tile_ref), channel_id=1, source_target_pairs={{0,3},{1,0},{2,1},{3,2},{4,7},{5,4},{6,5},{7,6},{8,11},{9,8},{10,9... | collective-permute-start | bytes 245768 | tf_op jit(solution)/shard_map/ppermute | solution.py:292
  6.5 7.7 %collective-permute-start.1 = (f32[40,512]{1,0:T(8,128)S(1)}, f32[40,512]{1,0:T(8,128)S(1)}, u32[]{:S(2)}, u32[]{:S(2)}) collective-permute-start(f32[40,512]{1,0:T(8,128)S(1)} %shard_map.76.tile_ref), channel_id=1, source_target_pairs={{0,2},{1,3},{2,0},{3,1},{4,6},{5,7},{6,4},{7,5},{8,10},{9,11},{10,... | collective-permute-start | bytes 245768 | tf_op jit(solution)/shard_map/ppermute | solution.py:292
  6.5 7.7 %collective-permute-start = (f32[40,512]{1,0:T(8,128)S(1)}, f32[40,512]{1,0:T(8,128)S(1)}, u32[]{:S(2)}, u32[]{:S(2)}) collective-permute-start(f32[40,512]{1,0:T(8,128)S(1)} %shard_map.76.tile_ref), channel_id=1, source_target_pairs={{0,1},{1,2},{2,3},{3,0},{4,5},{5,6},{6,7},{7,4},{8,9},{9,10},{10,1... | collective-permute-start | bytes 245768 | tf_op jit(solution)/shard_map/ppermute | solution.py:292
  14.2 18.3 %copy-start.1 = (f32[12,3,512]{2,1,0:T(4,128)S(1)}, f32[12,3,512]{2,1,0:T(4,128)}, u32[]{:S(2)}) copy-start(f32[12,3,512]{2,1,0:T(4,128)} %panels_ref.3) | copy-start | bytes 221188
  14.2 18.3 %copy-start.3 = (f32[3,3,512]{2,1,0:T(4,128)S(1)}, f32[3,3,512]{2,1,0:T(4,128)}, u32[]{:S(2)}) copy-start(f32[3,3,512]{2,1,0:T(4,128)} %normals_ref.1) | copy-start | bytes 55300
  14.2 18.3 %collective-permute-start.4 = (f32[4,40,512]{2,1,0:T(8,128)S(1)}, f32[4,40,512]{2,1,0:T(8,128)S(1)}, u32[]{:S(2)}, u32[]{:S(2)}) collective-permute-start(f32[4,40,512]{2,1,0:T(8,128)S(1)} %pad_maximum_fusion.tiles_ref), channel_id=1, source_target_pairs={{4,0},{8,4},{12,8},{16,12},{20,16},{24,20},{28,24},{5,1},{9,5},{13... | collective-permute-start | bytes 983048 | tf_op jit(solution)/shard_map/ppermute | solution.py:332
  17.0 15.4 %collective-permute-start.3 = (f32[4,40,512]{2,1,0:T(8,128)S(1)}, f32[4,40,512]{2,1,0:T(8,128)S(1)}, u32[]{:S(2)}, u32[]{:S(2)}) collective-permute-start(f32[4,40,512]{2,1,0:T(8,128)S(1)} %pad_maximum_fusion.tiles_ref), channel_id=1, source_target_pairs={{0,4},{4,8},{8,12},{12,16},{16,20},{20,24},{24,28},{1,5},{5,9},{9,... | collective-permute-start | bytes 983048 | tf_op jit(solution)/shard_map/ppermute | solution.py:331
  32.4 9.9 %copy-start.4 = (f32[2,512]{1,0:T(2,128)S(1)}, f32[2,512]{1,0:T(2,128)}, u32[]{:S(2)}) copy-start(f32[2,512]{1,0:T(2,128)} %state_ref.1) | copy-start | bytes 12292
  39.0 8.8 %collective-permute-start.7 = (f32[3,8,128]{2,1,0:T(8,128)S(1)}, f32[3,8,128]{2,1,0:T(8,128)S(1)}, u32[]{:S(2)}, u32[]{:S(2)}) collective-permute-start(f32[3,8,128]{2,1,0:T(8,128)S(1)} %get-tuple-element.6), channel_id=1, source_target_pairs={{0,3},{1,0},{2,1},{3,2},{4,7},{5,4},{6,5},{7,6},{8,11},{9,8},{10,9... | collective-permute-start | bytes 36872 | tf_op jit(solution)/shard_map/ppermute | solution.py:292
  40.8 6.9 %collective-permute-start.6 = (f32[3,8,128]{2,1,0:T(8,128)S(1)}, f32[3,8,128]{2,1,0:T(8,128)S(1)}, u32[]{:S(2)}, u32[]{:S(2)}) collective-permute-start(f32[3,8,128]{2,1,0:T(8,128)S(1)} %get-tuple-element.6), channel_id=1, source_target_pairs={{0,1},{1,2},{2,3},{3,0},{4,5},{5,6},{6,7},{7,4},{8,9},{9,10},{10,1... | collective-permute-start | bytes 36872 | tf_op jit(solution)/shard_map/ppermute | solution.py:292
  40.8 6.9 %collective-permute-start.5 = (f32[3,8,128]{2,1,0:T(8,128)S(1)}, f32[3,8,128]{2,1,0:T(8,128)S(1)}, u32[]{:S(2)}, u32[]{:S(2)}) collective-permute-start(f32[3,8,128]{2,1,0:T(8,128)S(1)} %get-tuple-element.6), channel_id=1, source_target_pairs={{0,2},{1,3},{2,0},{3,1},{4,6},{5,7},{6,4},{7,5},{8,10},{9,11},{10,... | collective-permute-start | bytes 36872 | tf_op jit(solution)/shard_map/ppermute | solution.py:292

commit v2 on v1

v2 whole, which is shorter than its diff:
```python
import functools

import jax
import jax.numpy as jnp
from jax import lax
from jax.experimental import pallas as pl
from jax.experimental.pallas import tpu as pltpu
from jax.sharding import PartitionSpec as P

soften = 0.01
gravity = 9.81
time_step = 0.2
mid_depth = -1.5
half = jnp.bfloat16
full = jnp.float32
DEPTH = 48


def rows_of(block_shape, rows):
    index = lax.broadcasted_iota(jnp.int32, block_shape, 0)
    block = jnp.zeros(block_shape, full)
    for position, row in enumerate(rows):
        block = jnp.where(index == position, row, block)
    return block


def three_parts(block):
    first = block.astype(half).astype(full)
    rest = block - first
    second = rest.astype(half).astype(full)
    return first, second, rest - second


def source_features(x, y, z):
    norm = x * x + y * y + z * z
    a, b, c = three_parts(rows_of((8, x.shape[1]), (x, y, z, norm, 1.0)))
    return jnp.concatenate([a, b, a, b, c, a], axis=0).T.astype(half)


def target_features(x, y, z):
    norm = x * x + y * y + z * z + soften
    a, b, c = three_parts(rows_of((8, x.shape[1]), (-2.0 * x, -2.0 * y, -2.0 * z, 1.0, norm)))
    return jnp.concatenate([a, a, b, b, a, c], axis=0).astype(half)


def two_parts(block):
    first = block.astype(half)
    return first, (block - first.astype(full)).astype(half)


def split_weights(block):
    first = block.astype(half).astype(full)
    return jnp.concatenate([first, block - first], axis=0).astype(half)


def product(left, right):
    return jnp.dot(left, right, preferred_element_type=full)


def weighted_sum(values, weights):
    high, low = two_parts(values)
    both = product(
        jnp.concatenate([weights, weights], axis=1), jnp.concatenate([high, low], axis=0)
    )
    return both[:8] + both[8:]


def influence_sum(targets, sources, weights):
    return weighted_sum(lax.rsqrt(product(sources, targets)), weights)


def point_row(bodies, member, axis):
    return 8 * bodies + 3 * member + axis


def surface_row(bodies, entry):
    return 11 * bodies + entry


def tile_rows(bodies):
    return -(-(11 * bodies + 3) // 8) * 8


def body_points(tile, bodies, member):
    return [
        tile[point_row(bodies, member, axis) : point_row(bodies, member, axis) + 1, :]
        for axis in range(3)
    ]


def surface_points(tile, bodies):
    x, y, weight = [
        tile[surface_row(bodies, entry) : surface_row(bodies, entry) + 1, :] for entry in range(3)
    ]
    return x, y, jnp.full_like(x, -mid_depth), weight


def pack_kernel(panels_hbm, surface_hbm, tile_ref, panels_ref, surface_ref, sems):
    bodies = panels_ref.shape[1]
    copies = [
        pltpu.make_async_copy(panels_hbm, panels_ref, sems.at[0]),
        pltpu.make_async_copy(surface_hbm, surface_ref, sems.at[1]),
    ]
    for copy in copies:
        copy.start()
    base = lax.axis_index("body") * bodies
    tile_ref[...] = jnp.zeros_like(tile_ref)
    for copy in copies:
        copy.wait()
    area = panels_ref[3]
    for member in range(bodies):
        for entry in range(8):
            tile_ref[8 * member + entry : 8 * member + entry + 1, :] = (
                panels_ref[4 + entry, member : member + 1, :] * area[member : member + 1, :]
            )
        centre = (2 * (base + member)).astype(full)
        for axis, shift in enumerate((centre, 0.0, mid_depth)):
            row = point_row(bodies, member, axis)
            tile_ref[row : row + 1, :] = panels_ref[axis, member : member + 1, :] - shift
    group_centre = (2 * base + (bodies - 1)).astype(full)
    row = surface_row(bodies, 0)
    tile_ref[row : row + 1, :] = surface_ref[0:1, :] - group_centre
    tile_ref[row + 1 : row + 2, :] = surface_ref[1:2, :]
    tile_ref[row + 2 : row + 3, :] = surface_ref[2:3, :] * surface_ref[3:4, :]


def body_weights(tile, member):
    return split_weights(tile[8 * member : 8 * member + 8, :])


def moment_weights(tile, bodies, member):
    x, y, z = body_points(tile, bodies, member)
    first = tile[8 * member : 8 * member + 1, :]
    return split_weights(rows_of((8, x.shape[1]), (first, first * x, first * y, first * z)))


def prepare_tile(tile, bodies, columns, features, weights, spread):
    for member in range(bodies):
        features[member, columns, :] = source_features(*body_points(tile, bodies, member))
        weights[member, :, columns] = body_weights(tile, member)
    x, y, z, weight = surface_points(tile, bodies)
    features[bodies, columns, :] = source_features(x, y, z)
    spread[columns, :] = jnp.broadcast_to(weight, (128, x.shape[1])).T


def surface_sum(targets, sources, spread):
    values = lax.rsqrt(product(sources, targets))
    count, width = values.shape
    sums = []
    for start in range(0, width, 128):
        term = values[:, start : start + 128] * spread
        sums.append(jnp.sum(term.reshape(count // 8, 8, 128), axis=0))
    return jnp.sum(jnp.concatenate(sums, axis=1), axis=0, keepdims=True)


def velocity_term(features, weights, place, y, z):
    inverse = lax.rsqrt(product(features, target_features(place, y, z)))
    moments = weighted_sum(inverse * inverse * inverse, weights)
    return [
        moments[axis + 1 : axis + 2] - at * moments[0:1] for axis, at in enumerate((place, y, z))
    ]


def targets_of(points, member, shift):
    block = points[member]
    return target_features(block[0:1] + shift, block[1:2], block[2:3])


def group_sums(bodies, edges, inner, points, features, weights, spread, acc_ref):
    def own_step(member, carry):
        acc_ref[member] += influence_sum(
            targets_of(points, member, 0.0), features[member], weights[member]
        )
        shift = (2 * member - (bodies - 1)).astype(full)
        acc_ref[member, 0:1, :] += surface_sum(
            targets_of(points, member, shift), features[bodies], spread[...]
        )
        return carry

    lax.fori_loop(0, bodies, own_step, 0)
    inner()

    def pair_step(step, carry):
        target, source = edges[0, step], edges[1, step]
        shift = (2 * (target - source)).astype(full)
        acc_ref[target] += influence_sum(
            targets_of(points, target, shift), features[source], weights[source]
        )
        return carry

    lax.fori_loop(0, edges[4, 0], pair_step, 0)


def own_tile_kernel(
    bodies, pairs_hbm, tile_ref, acc_ref, velocity_ref, edges,
    features, weights, spread, points, pairs, sem,
):
    width = tile_ref.shape[1]
    copy = pltpu.make_async_copy(pairs_hbm, pairs, sem)
    copy.start()
    tile = tile_ref[...]
    prepare_tile(tile, bodies, pl.ds(0, width), features, weights, spread)
    for member in range(bodies):
        points[member] = rows_of((8, width), body_points(tile, bodies, member))
    acc_ref[...] = jnp.zeros_like(acc_ref)
    base = lax.axis_index("body") * bodies

    def list_edges():
        copy.wait()
        for slot in range(2 + 2 * bodies):
            edges[4, slot] = 0

        def step_edge(step, carry):
            target = pairs[step % 2, step // 2] - base
            source = pairs[1 - step % 2, step // 2] - base

            @pl.when((target >= 0) & (target < bodies))
            def _():
                inside = (source >= 0) & (source < bodies)
                row = jnp.where(inside, 0, 1)
                place = edges[4, row]
                edges[2 * row, place] = target
                edges[2 * row + 1, place] = source
                edges[4, row] = place + 1

                @pl.when(jnp.logical_not(inside))
                def _():
                    edges[4, 2 + jnp.where(source < 0, source + bodies, source)] = 1

            return carry

        lax.fori_loop(0, 2 * pairs.shape[1], step_edge, 0)

    group_sums(bodies, edges, list_edges, points, features, weights, spread, acc_ref)
    x, y, z, _ = surface_points(tile, bodies)
    total = [jnp.zeros((1, width), full)] * 3
    for member in range(bodies):
        term = velocity_term(
            features[member], moment_weights(tile, bodies, member), x + float(bodies - 1 - 2 * member), y, z
        )
        total = [so_far + part for so_far, part in zip(total, term)]
    velocity_ref[...] = rows_of((8, width), total)


def group_kernel(
    bodies, edges_hbm, tiles_ref, given_ref, acc_ref, features, weights, spread, points, edges, sem
):
    count, _, width = tiles_ref.shape
    copy = pltpu.make_async_copy(edges_hbm, edges, sem)
    copy.start()
    for index in range(1, count):
        columns = pl.ds((index - 1) * width, width)
        prepare_tile(tiles_ref[index], bodies, columns, features, weights, spread)
    own = tiles_ref[0]
    for member in range(bodies):
        points[member] = rows_of((8, width), body_points(own, bodies, member))
    acc_ref[...] = given_ref[...]
    group_sums(bodies, edges, copy.wait, points, features, weights, spread, acc_ref)


def crossing_kernel(
    bodies, edges_hbm, lower_ref, upper_ref, tile_ref, panels_ref, normals_ref, given_ref,
    potential_hbm, force_ref, acc_ref, features, weights, points, edges, sems,
):
    count, _, width = lower_ref.shape
    copy = pltpu.make_async_copy(edges_hbm, edges, sems.at[0])
    copy.start()
    own = tile_ref[...]
    for member in range(bodies):
        points[member] = rows_of((8, width), body_points(own, bodies, member))
    acc_ref[...] = given_ref[...]
    force_ref[...] = jnp.zeros_like(force_ref)
    copy.wait()
    for slot in range(2 * bodies):

        @pl.when(edges[4, 2 + slot] == 1)
        def _():
            side = lower_ref if slot < bodies else upper_ref
            for index in range(count):
                columns = pl.ds(index * width, width)
                tile = side[index]
                member = slot % bodies
                features[slot, columns, :] = source_features(*body_points(tile, bodies, member))
                weights[slot, :, columns] = body_weights(tile, member)

    def pair_step(step, carry):
        target, source = edges[2, step], edges[3, step]
        shift = (2 * (target - source)).astype(full)
        slot = jnp.where(source < 0, source + bodies, source)
        acc_ref[target] += influence_sum(
            targets_of(points, target, shift), features[slot], weights[slot]
        )
        return carry

    lax.fori_loop(0, edges[4, 1], pair_step, 0)
    store = pltpu.make_async_copy(acc_ref, potential_hbm, sems.at[1])
    store.start()
    for member in range(bodies):
        area = panels_ref[3, member : member + 1, :]
        scaled = rows_of(
            (8, width), [normals_ref[axis, member : member + 1, :] * area for axis in range(3)]
        )
        force_ref[member, :, 0:8] = lax.dot_general(
            scaled,
            acc_ref[member],
            (((1,), (1,)), ((), ())),
            precision=lax.Precision.HIGHEST,
            preferred_element_type=full,
        )
    store.wait()


def velocity_kernel(bodies, tiles_ref, features, given_ref, state_ref, next_ref, weights):
    count, _, width = tiles_ref.shape
    for index in range(1, count):
        tile = tiles_ref[index]
        for member in range(bodies):
            weights[member, :, pl.ds((index - 1) * width, width)] = moment_weights(
                tile, bodies, member
            )
    own = tiles_ref[0]
    x, y, z, _ = surface_points(own, bodies)

    def body_step(member, velocity):
        place = x + (bodies - 1 - 2 * member).astype(full)
        term = velocity_term(features[member], weights[member], place, y, z)
        return tuple(so_far + part for so_far, part in zip(velocity, term))

    start = tuple(given_ref[axis : axis + 1, :] for axis in range(3))
    velocity = lax.fori_loop(0, bodies, body_step, start)
    speed_sq = velocity[0] * velocity[0] + velocity[1] * velocity[1] + velocity[2] * velocity[2]
    potential, elevation = state_ref[0:1, :], state_ref[1:2, :]
    next_ref[0:1, :] = potential + time_step * (-gravity * elevation - 0.5 * speed_sq)
    next_ref[1:2, :] = elevation + time_step * velocity[2]


VMEM, SMEM, ANY = pltpu.VMEM, pltpu.SMEM, pl.ANY


def call(kernel, operands, results, scratch=(), units=0.0):
    single = len(results) == 1
    out = pl.pallas_call(
        kernel,
        out_shape=[jax.ShapeDtypeStruct(shape, kind) for _, shape, kind in results],
        in_specs=[pl.BlockSpec(memory_space=space) for space, _ in operands],
        out_specs=[pl.BlockSpec(memory_space=space) for space, _, _ in results],
        scratch_shapes=list(scratch),
        compiler_params=pltpu.CompilerParams(vmem_limit_bytes=40 * 1024 * 1024),
        cost_estimate=pl.CostEstimate(
            flops=int(units * 1.2e9), bytes_accessed=1024, transcendentals=0
        ),
    )(*[array for _, array in operands])
    return out[0] if single else out


def rotations(block, axis):
    count = lax.axis_size(axis)
    return [
        lax.ppermute(block, axis, [(i, (i + k) % count) for i in range(count)])
        for k in range(1, count)
    ]


def on_device(body_panels, body_normals, fs_panels, fs_state, pairs):
    bodies = body_panels.shape[1]
    width = body_panels.shape[2]
    tiles_count = lax.axis_size("surf")
    groups = lax.axis_size("body")
    semaphore = pltpu.SemaphoreType.DMA
    own = call(
        pack_kernel,
        [(ANY, body_panels), (ANY, fs_panels)],
        [(VMEM, (tile_rows(bodies), width), full)],
        scratch=(VMEM(body_panels.shape, full), VMEM(fs_panels.shape, full), semaphore((2,))),
    )
    if tiles_count == 4:
        tiles = jnp.stack([own] + rotations(own, "surf"))
    else:
        everything = lax.all_gather(own, "surf")
        tiles = jnp.concatenate(
            [own[None]]
            + [
                lax.dynamic_index_in_dim(
                    everything, (lax.axis_index("surf") + k) % tiles_count, 0
                )
                for k in range(1, tiles_count)
            ]
        )
    wide = width * tiles_count
    rest = wide - width
    acc_shape = (bodies, 8, width)
    edges_shape = (5, max(2 * pairs.shape[0], 2 + 2 * bodies))
    points = VMEM(acc_shape, full)
    edges_space = SMEM(edges_shape, jnp.int32)
    partial, velocity, edges = call(
        functools.partial(own_tile_kernel, bodies),
        [(ANY, pairs.T), (VMEM, own)],
        [
            (VMEM, acc_shape, full),
            (VMEM, (8, width), full),
            (SMEM, edges_shape, jnp.int32),
        ],
        scratch=(
            VMEM((bodies + 1, width, DEPTH), half),
            VMEM((bodies, 16, width), half),
            VMEM((width, 128), full),
            points,
            SMEM((2, pairs.shape[0]), jnp.int32),
            semaphore,
        ),
        units=3.0,
    )
    lower = lax.ppermute(tiles, "body", [(i, i + 1) for i in range(groups - 1)])
    upper = lax.ppermute(tiles, "body", [(i + 1, i) for i in range(groups - 1)])
    partial, features = call(
        functools.partial(group_kernel, bodies),
        [(ANY, edges), (VMEM, tiles), (VMEM, partial)],
        [(VMEM, acc_shape, full), (VMEM, (bodies + 1, rest, DEPTH), half)],
        scratch=(
            VMEM((bodies, 16, rest), half),
            VMEM((rest, 128), full),
            points,
            edges_space,
            semaphore,
        ),
        units=7.0,
    )
    own_potential, force = call(
        functools.partial(crossing_kernel, bodies),
        [(ANY, edges), (VMEM, lower), (VMEM, upper), (VMEM, own), (VMEM, body_panels),
         (VMEM, body_normals), (VMEM, partial)],
        [(ANY, acc_shape, full), (VMEM, (bodies, 8, 128), full)],
        scratch=(
            VMEM(acc_shape, full),
            VMEM((2 * bodies, wide, DEPTH), half),
            VMEM((2 * bodies, 16, wide), half),
            points,
            edges_space,
            semaphore((2,)),
        ),
        units=6.0,
    )
    fs_next = call(
        functools.partial(velocity_kernel, bodies),
        [(VMEM, tiles), (VMEM, features), (VMEM, velocity), (VMEM, fs_state)],
        [(VMEM, (2, width), full)],
        scratch=(VMEM((bodies, 16, rest), half),),
        units=5.0,
    )
    if tiles_count == 4:
        first, second, third = rotations(force, "surf")
        total = (force + second) + (first + third)
    else:
        total = lax.psum(force, "surf")
    return own_potential, total[:, :3, :8].transpose(0, 2, 1), fs_next


def solution(mesh):
    placed = (
        P(None, "body", "surf"),
        P(None, "body", "surf"),
        P(None, ("body", "surf")),
        P(None, ("body", "surf")),
        P(),
    )
    return jax.shard_map(
        on_device,
        mesh=mesh,
        in_specs=placed,
        out_specs=(P("body", None, "surf"), P("body", None, None), P(None, ("body", "surf"))),
        check_vma=False,
    )
```

time: 49.4 us -> 45.1 us (0.913)
  the two profiles are of different devices: /device:TPU:1 before, /device:TPU:2 now
where the time goes in v2:
time: 45.1 us; the launch traced here: 44.9 us
  Pallas kernels  25.8 us (57%)
  starting transfers between devices  15.4 us (34%)
  local copies, waits for them, and re-layouts  2.28 us (5%)
  between operations  0.78 us (2%)
  other arithmetic  0.62 us (1%)
    pallas_call x5, Pallas kernels, call(): pl.pallas_call(kernel, out_shape=[jax.ShapeDtypeStruct(shape, kind) for _...  25.8 us
    ppermute x6, starting transfers between devices, rotations(): lax.ppermute(block, axis, [(i, (i + k) % count) for i in range(count)])  9.81 us
    ppermute x1, starting transfers between devices, on_device(): upper = lax.ppermute(tiles, 'body', [(i + 1, i) for i in range(groups - 1)])  3.64 us
    unnamed x12, local copies, waits for them, and re-layouts  2.28 us
    ppermute x1, starting transfers between devices, on_device(): lower = lax.ppermute(tiles, 'body', [(i, i + 1) for i in range(groups - 1)])  1.92 us
  transfers between devices with their start and end apart: 8, of which 0 were waited for; matrix products, arithmetic and copies ran while one was open for 0% of the time, Pallas kernels for 36%

profile of v2, /device:TPU:2, one launch (start us, length us, event | category | flops | bytes accessed | tf_op | source)
XLA Modules:
  0.0 44.9 jit_solution(2060370769516945523)
XLA Ops:
  0.6 0.0 copy-start
  0.6 0.9 %copy-done = f32[12,3,512]{2,1,0:T(4,128)S(1)} copy-done((f32[12,3,512]{2,1,0:T(4,128)S(1)}, f32[12,3,512]{2,1,0:T(4,128)}, u32[]{:S(2)}) %copy-start) | copy-done | bytes 73752
  1.5 0.0 copy-start.2
  1.5 0.7 %copy-done.2 = f32[4,512]{1,0:T(4,128)S(1)} copy-done((f32[4,512]{1,0:T(4,128)S(1)}, f32[4,512]{1,0:T(4,128)}, u32[]{:S(2)}) %copy-start.2) | copy-done | bytes 8216
  2.2 0.2 shard_map.76.tile_ref
  2.4 1.6 %collective-permute-start = (f32[40,512]{1,0:T(8,128)S(1)}, f32[40,512]{1,0:T(8,128)S(1)}, u32[]{:S(2)}, u32[]{:S(2)}) collective-permute-start(f32[40,512]{1,0:T(8,128)S(1)} %shard_map.76.tile_ref), channel_id=1, source_target_pairs={{0,1},{1,2},{2,3},{3,0},{4,5},{5,6},{6,7},{7,4},{8,9},{9,10},{10,1... | collective-permute-start | bytes 245768 | tf_op jit(solution)/shard_map/ppermute | solution.py:359
  4.0 2.6 %collective-permute-start.1 = (f32[40,512]{1,0:T(8,128)S(1)}, f32[40,512]{1,0:T(8,128)S(1)}, u32[]{:S(2)}, u32[]{:S(2)}) collective-permute-start(f32[40,512]{1,0:T(8,128)S(1)} %shard_map.76.tile_ref), channel_id=1, source_target_pairs={{0,2},{1,3},{2,0},{3,1},{4,6},{5,7},{6,4},{7,5},{8,10},{9,11},{10,... | collective-permute-start | bytes 245768 | tf_op jit(solution)/shard_map/ppermute | solution.py:359
  6.6 1.3 %collective-permute-start.2 = (f32[40,512]{1,0:T(8,128)S(1)}, f32[40,512]{1,0:T(8,128)S(1)}, u32[]{:S(2)}, u32[]{:S(2)}) collective-permute-start(f32[40,512]{1,0:T(8,128)S(1)} %shard_map.76.tile_ref), channel_id=1, source_target_pairs={{0,3},{1,0},{2,1},{3,2},{4,7},{5,4},{6,5},{7,6},{8,11},{9,8},{10,9... | collective-permute-start | bytes 245768 | tf_op jit(solution)/shard_map/ppermute | solution.py:359
  8.0 0.0 copy-start.5
  8.0 0.7 %copy-done.5 = s32[18,2]{0,1:T(2,128)S(1)} copy-done((s32[18,2]{0,1:T(2,128)S(1)}, s32[18,2]{0,1:T(2,128)}, u32[]{:S(2)}) %copy-start.5) | copy-done | bytes 168
  8.6 5.4 %shard_map.77 = (f32[3,8,512]{2,1,0:T(8,128)S(1)}, f32[8,512]{1,0:T(8,128)S(1)}, s32[5,36]{1,0:T(8,128)S(1)}) custom-call(s32[2,18]{1,0:T(2,128)S(1)} %bitcast.8, f32[40,512]{1,0:T(8,128)S(1)} %shard_map.76.tile_ref), custom_call_target="tpu_custom_call" | custom-call | flops 3600000000 | bytes 1024 | tf_op jit(solution)/shard_map/pallas_call | solution.py:342
  14.1 0.0 collective-permute-done
  14.1 0.0 collective-permute-done.1
  14.1 0.0 collective-permute-done.2
  14.1 1.9 %collective-permute-start.3 = (f32[4,40,512]{2,1,0:T(8,128)S(1)}, f32[4,40,512]{2,1,0:T(8,128)S(1)}, u32[]{:S(2)}, u32[]{:S(2)}) collective-permute-start(f32[4,40,512]{2,1,0:T(8,128)S(1)} %pad_maximum_fusion.tiles_ref), channel_id=1, source_target_pairs={{0,4},{4,8},{8,12},{12,16},{16,20},{20,24},{24,28},{1,5},{5,9},{9,... | collective-permute-start | bytes 983048 | tf_op jit(solution)/shard_map/ppermute | solution.py:413
  16.0 3.6 %collective-permute-start.4 = (f32[4,40,512]{2,1,0:T(8,128)S(1)}, f32[4,40,512]{2,1,0:T(8,128)S(1)}, u32[]{:S(2)}, u32[]{:S(2)}) collective-permute-start(f32[4,40,512]{2,1,0:T(8,128)S(1)} %pad_maximum_fusion.tiles_ref), channel_id=1, source_target_pairs={{4,0},{8,4},{12,8},{16,12},{20,16},{24,20},{28,24},{5,1},{9,5},{13... | collective-permute-start | bytes 983048 | tf_op jit(solution)/shard_map/ppermute | solution.py:414
  19.7 0.0 copy-start.1
  19.7 0.0 copy-start.3
  19.7 6.8 %shard_map.78 = (f32[3,8,512]{2,1,0:T(8,128)S(1)}, bf16[4,1536,48]{2,1,0:T(8,128)(2,1)S(1)}) custom-call(s32[5,36]{1,0:T(8,128)S(1)} %get-tuple-element.10.edges_hbm, f32[4,40,512]{2,1,0:T(8,128)S(1)} %pad_maximum_fusion.tiles_ref, f32[3,8,512]{2,1,0:T(8,128)S(1)} %get-tuple-element.11.given_ref), custom_call_target="tpu_custom_call" | custom-call | flops 8400000000 | bytes 1024 | tf_op jit(solution)/shard_map/pallas_call | solution.py:342
  26.5 0.0 collective-permute-done.3.lower_ref
  26.5 0.0 collective-permute-done.4.upper_ref
  26.5 0.0 copy-done.1
  26.5 0.0 copy-done.3
  26.5 0.0 copy-start.4
  26.5 9.6 %shard_map.79 = (f32[3,8,512]{2,1,0:T(8,128)}, f32[3,8,128]{2,1,0:T(8,128)S(1)}) custom-call(s32[5,36]{1,0:T(8,128)S(1)} %get-tuple-element.10.edges_hbm, f32[4,40,512]{2,1,0:T(8,128)S(1)} %collective-permute-done.3.lower_ref, f32[4,40,512]{2,1,0:T(8,128)S(1)} %collective-permute-done.4.upper_ref, f32[40,512]{1,0:T(8,128)S(1)} %shard_map.76.tile_ref, ...), custom_call_target="tpu_custom_call" | custom-call | flops 7200000000 | bytes 1024 | tf_op jit(solution)/shard_map/pallas_call | solution.py:342
  36.1 0.4 collective-permute-start.5
  36.5 1.7 %collective-permute-start.6 = (f32[3,8,128]{2,1,0:T(8,128)S(1)}, f32[3,8,128]{2,1,0:T(8,128)S(1)}, u32[]{:S(2)}, u32[]{:S(2)}) collective-permute-start(f32[3,8,128]{2,1,0:T(8,128)S(1)} %get-tuple-element.14), channel_id=1, source_target_pairs={{0,1},{1,2},{2,3},{3,0},{4,5},{5,6},{6,7},{7,4},{8,9},{9,10},{10,1... | collective-permute-start | bytes 36872 | tf_op jit(solution)/shard_map/ppermute | solution.py:359
  38.3 2.1 %collective-permute-start.7 = (f32[3,8,128]{2,1,0:T(8,128)S(1)}, f32[3,8,128]{2,1,0:T(8,128)S(1)}, u32[]{:S(2)}, u32[]{:S(2)}) collective-permute-start(f32[3,8,128]{2,1,0:T(8,128)S(1)} %get-tuple-element.14), channel_id=1, source_target_pairs={{0,3},{1,0},{2,1},{3,2},{4,7},{5,4},{6,5},{7,6},{8,11},{9,8},{10,9... | collective-permute-start | bytes 36872 | tf_op jit(solution)/shard_map/ppermute | solution.py:359
  40.4 0.0 copy-done.4
  40.4 3.9 %shard_map.80 = f32[2,512]{1,0:T(2,128)} custom-call(f32[4,40,512]{2,1,0:T(8,128)S(1)} %pad_maximum_fusion.tiles_ref, bf16[4,1536,48]{2,1,0:T(8,128)(2,1)S(1)} %get-tuple-element.15.features, f32[8,512]{1,0:T(8,128)S(1)} %get-tuple-element.16.given_ref, f32[2,512]{1,0:T(2,128)S(1)} %copy-done.4), custom_call_target="tpu_custom_call" | custom-call | flops 6000000000 | bytes 1024 | tf_op jit(solution)/shard_map/pallas_call | solution.py:342
  44.3 0.0 collective-permute-done.5
  44.3 0.0 collective-permute-done.6
  44.3 0.0 collective-permute-done.7
  44.3 0.6 %fusion.1 = f32[3,8,3]{1,2,0:T(4,128)} fusion(f32[3,8,128]{2,1,0:T(8,128)S(1)} %collective-permute-done.7, f32[3,8,128]{2,1,0:T(8,128)S(1)} %collective-permute-done.6, f32[3,8,128]{2,1,0:T(8,128)S(1)} %collective-permute-done.5, f32[3,8,128]{2,1,0:T(8,128)S(1)} %get-tuple-element.14), kind=kLoop, calls=%fused_computation.3 | loop fusion | flops 216 | bytes 1440 | tf_op jit(solution)/shard_map/transpose | solution.py:455
  (1 shorter events, 0.0 us)
Async XLA Ops:
  0.6 0.9 %copy-start = (f32[12,3,512]{2,1,0:T(4,128)S(1)}, f32[12,3,512]{2,1,0:T(4,128)}, u32[]{:S(2)}) copy-start(f32[12,3,512]{2,1,0:T(4,128)} %panels_ref.1) | copy-start | bytes 221188
  1.5 0.7 %copy-start.2 = (f32[4,512]{1,0:T(4,128)S(1)}, f32[4,512]{1,0:T(4,128)}, u32[]{:S(2)}) copy-start(f32[4,512]{1,0:T(4,128)} %surface_hbm.1) | copy-start | bytes 24580
  2.4 11.7 %collective-permute-start = (f32[40,512]{1,0:T(8,128)S(1)}, f32[40,512]{1,0:T(8,128)S(1)}, u32[]{:S(2)}, u32[]{:S(2)}) collective-permute-start(f32[40,512]{1,0:T(8,128)S(1)} %shard_map.76.tile_ref), channel_id=1, source_target_pairs={{0,1},{1,2},{2,3},{3,0},{4,5},{5,6},{6,7},{7,4},{8,9},{9,10},{10,1... | collective-permute-start | bytes 245768 | tf_op jit(solution)/shard_map/ppermute | solution.py:359
  4.0 10.1 %collective-permute-start.1 = (f32[40,512]{1,0:T(8,128)S(1)}, f32[40,512]{1,0:T(8,128)S(1)}, u32[]{:S(2)}, u32[]{:S(2)}) collective-permute-start(f32[40,512]{1,0:T(8,128)S(1)} %shard_map.76.tile_ref), channel_id=1, source_target_pairs={{0,2},{1,3},{2,0},{3,1},{4,6},{5,7},{6,4},{7,5},{8,10},{9,11},{10,... | collective-permute-start | bytes 245768 | tf_op jit(solution)/shard_map/ppermute | solution.py:359
  6.6 7.5 %collective-permute-start.2 = (f32[40,512]{1,0:T(8,128)S(1)}, f32[40,512]{1,0:T(8,128)S(1)}, u32[]{:S(2)}, u32[]{:S(2)}) collective-permute-start(f32[40,512]{1,0:T(8,128)S(1)} %shard_map.76.tile_ref), channel_id=1, source_target_pairs={{0,3},{1,0},{2,1},{3,2},{4,7},{5,4},{6,5},{7,6},{8,11},{9,8},{10,9... | collective-permute-start | bytes 245768 | tf_op jit(solution)/shard_map/ppermute | solution.py:359
  8.0 0.7 %copy-start.5 = (s32[18,2]{0,1:T(2,128)S(1)}, s32[18,2]{0,1:T(2,128)}, u32[]{:S(2)}) copy-start(s32[18,2]{0,1:T(2,128)} %param.9) | copy-start | bytes 436
  14.1 12.4 %collective-permute-start.3 = (f32[4,40,512]{2,1,0:T(8,128)S(1)}, f32[4,40,512]{2,1,0:T(8,128)S(1)}, u32[]{:S(2)}, u32[]{:S(2)}) collective-permute-start(f32[4,40,512]{2,1,0:T(8,128)S(1)} %pad_maximum_fusion.tiles_ref), channel_id=1, source_target_pairs={{0,4},{4,8},{8,12},{12,16},{16,20},{20,24},{24,28},{1,5},{5,9},{9,... | collective-permute-start | bytes 983048 | tf_op jit(solution)/shard_map/ppermute | solution.py:413
  16.0 10.4 %collective-permute-start.4 = (f32[4,40,512]{2,1,0:T(8,128)S(1)}, f32[4,40,512]{2,1,0:T(8,128)S(1)}, u32[]{:S(2)}, u32[]{:S(2)}) collective-permute-start(f32[4,40,512]{2,1,0:T(8,128)S(1)} %pad_maximum_fusion.tiles_ref), channel_id=1, source_target_pairs={{4,0},{8,4},{12,8},{16,12},{20,16},{24,20},{28,24},{5,1},{9,5},{13... | collective-permute-start | bytes 983048 | tf_op jit(solution)/shard_map/ppermute | solution.py:414
  19.7 6.8 %copy-start.1 = (f32[12,3,512]{2,1,0:T(4,128)S(1)}, f32[12,3,512]{2,1,0:T(4,128)}, u32[]{:S(2)}) copy-start(f32[12,3,512]{2,1,0:T(4,128)} %panels_ref.1) | copy-start | bytes 221188
  19.7 6.8 %copy-start.3 = (f32[3,3,512]{2,1,0:T(4,128)S(1)}, f32[3,3,512]{2,1,0:T(4,128)}, u32[]{:S(2)}) copy-start(f32[3,3,512]{2,1,0:T(4,128)} %normals_ref.1) | copy-start | bytes 55300
  26.5 13.9 %copy-start.4 = (f32[2,512]{1,0:T(2,128)S(1)}, f32[2,512]{1,0:T(2,128)}, u32[]{:S(2)}) copy-start(f32[2,512]{1,0:T(2,128)} %state_ref.1) | copy-start | bytes 12292
  36.1 8.1 %collective-permute-start.5 = (f32[3,8,128]{2,1,0:T(8,128)S(1)}, f32[3,8,128]{2,1,0:T(8,128)S(1)}, u32[]{:S(2)}, u32[]{:S(2)}) collective-permute-start(f32[3,8,128]{2,1,0:T(8,128)S(1)} %get-tuple-element.14), channel_id=1, source_target_pairs={{0,2},{1,3},{2,0},{3,1},{4,6},{5,7},{6,4},{7,5},{8,10},{9,11},{10,... | collective-permute-start | bytes 36872 | tf_op jit(solution)/shard_map/ppermute | solution.py:359
  36.5 7.7 %collective-permute-start.6 = (f32[3,8,128]{2,1,0:T(8,128)S(1)}, f32[3,8,128]{2,1,0:T(8,128)S(1)}, u32[]{:S(2)}, u32[]{:S(2)}) collective-permute-start(f32[3,8,128]{2,1,0:T(8,128)S(1)} %get-tuple-element.14), channel_id=1, source_target_pairs={{0,1},{1,2},{2,3},{3,0},{4,5},{5,6},{6,7},{7,4},{8,9},{9,10},{10,1... | collective-permute-start | bytes 36872 | tf_op jit(solution)/shard_map/ppermute | solution.py:359
  38.3 6.0 %collective-permute-start.7 = (f32[3,8,128]{2,1,0:T(8,128)S(1)}, f32[3,8,128]{2,1,0:T(8,128)S(1)}, u32[]{:S(2)}, u32[]{:S(2)}) collective-permute-start(f32[3,8,128]{2,1,0:T(8,128)S(1)} %get-tuple-element.14), channel_id=1, source_target_pairs={{0,3},{1,0},{2,1},{3,2},{4,7},{5,4},{6,5},{7,6},{8,11},{9,8},{10,9... | collective-permute-start | bytes 36872 | tf_op jit(solution)/shard_map/ppermute | solution.py:359

commit v3 on v2

--- a/solution.py
+++ b/solution.py
@@ -166,114 +166,134 @@
     return target_features(block[0:1] + shift, block[1:2], block[2:3])
 
 
-def group_sums(bodies, edges, inner, points, features, weights, spread, acc_ref):
-    def own_step(member, carry):
-        acc_ref[member] += influence_sum(
-            targets_of(points, member, 0.0), features[member], weights[member]
-        )
-        shift = (2 * member - (bodies - 1)).astype(full)
-        acc_ref[member, 0:1, :] += surface_sum(
-            targets_of(points, member, shift), features[bodies], spread[...]
-        )
-        return carry
-
-    lax.fori_loop(0, bodies, own_step, 0)
-    inner()
-
-    def pair_step(step, carry):
-        target, source = edges[0, step], edges[1, step]
-        shift = (2 * (target - source)).astype(full)
-        acc_ref[target] += influence_sum(
-            targets_of(points, target, shift), features[source], weights[source]
-        )
-        return carry
-
-    lax.fori_loop(0, edges[4, 0], pair_step, 0)
+def code_rows(pair_count):
+    return 4 * pair_count + 1
 
 
 def own_tile_kernel(
-    bodies, pairs_hbm, tile_ref, acc_ref, velocity_ref, edges,
-    features, weights, spread, points, pairs, sem,
+    bodies, pairs_hbm, tile_ref, acc_ref, velocity_ref, features, codes,
+    weights, spread, pairs, counts, sem,
 ):
     width = tile_ref.shape[1]
     copy = pltpu.make_async_copy(pairs_hbm, pairs, sem)
     copy.start()
     tile = tile_ref[...]
     prepare_tile(tile, bodies, pl.ds(0, width), features, weights, spread)
-    for member in range(bodies):
-        points[member] = rows_of((8, width), body_points(tile, bodies, member))
-    acc_ref[...] = jnp.zeros_like(acc_ref)
-    base = lax.axis_index("body") * bodies
-
-    def list_edges():
-        copy.wait()
-        for slot in range(2 + 2 * bodies):
-            edges[4, slot] = 0
-
-        def step_edge(step, carry):
-            target = pairs[step % 2, step // 2] - base
-            source = pairs[1 - step % 2, step // 2] - base
-
-            @pl.when((target >= 0) & (target < bodies))
-            def _():
-                inside = (source >= 0) & (source < bodies)
-                row = jnp.where(inside, 0, 1)
-                place = edges[4, row]
-                edges[2 * row, place] = target
-                edges[2 * row + 1, place] = source
-                edges[4, row] = place + 1
-
-                @pl.when(jnp.logical_not(inside))
-                def _():
-                    edges[4, 2 + jnp.where(source < 0, source + bodies, source)] = 1
-
-            return carry
-
-        lax.fori_loop(0, 2 * pairs.shape[1], step_edge, 0)
-
-    group_sums(bodies, edges, list_edges, points, features, weights, spread, acc_ref)
     x, y, z, _ = surface_points(tile, bodies)
     total = [jnp.zeros((1, width), full)] * 3
-    for member in range(bodies):
+    index = lax.broadcasted_iota(jnp.int32, (8, width), 0)
+    for member in range(bodies):
+        point = body_points(tile, bodies, member)
+        self_part = influence_sum(target_features(*point), features[member], weights[member])
+        shift = float(2 * member - (bodies - 1))
+        surface_part = surface_sum(
+            target_features(point[0] + shift, point[1], point[2]), features[bodies], spread[...]
+        )
+        acc_ref[member] = self_part + jnp.where(index == 0, surface_part, 0.0)
         term = velocity_term(
-            features[member], moment_weights(tile, bodies, member), x + float(bodies - 1 - 2 * member), y, z
+            features[member], moment_weights(tile, bodies, member), x - shift, y, z
         )
         total = [so_far + part for so_far, part in zip(total, term)]
     velocity_ref[...] = rows_of((8, width), total)
 
+    base = lax.axis_index("body") * bodies
+    pair_count = pairs.shape[1]
+    copy.wait()
+    for entry in range(3):
+        counts[entry] = 0
+
+    def step_edge(step, carry):
+        target = pairs[step % 2, step // 2] - base
+        source = pairs[1 - step % 2, step // 2] - base
+
+        @pl.when((target >= 0) & (target < bodies))
+        def _():
+            inside = (source >= 0) & (source < bodies)
+            row = jnp.where(inside, 0, 1)
+            slot = jnp.where(source < 0, source + bodies, source)
+            place = counts[row]
+            codes[pl.ds(row * 2 * pair_count + place, 1), :] = jnp.full(
+                (1, 128), target * 16 + slot, jnp.int32
+            )
+            counts[row] = place + 1
+            counts[2] = counts[2] | jnp.where(inside, 0, jnp.left_shift(1, slot))
+
+        return carry
+
+    lax.fori_loop(0, 2 * pair_count, step_edge, 0)
+    lane = lax.broadcasted_iota(jnp.int32, (1, 128), 1)
+    codes[4 * pair_count : 4 * pair_count + 1, :] = jnp.where(
+        lane == 0, counts[0], jnp.where(lane == 1, counts[1], counts[2])
+    )
+
+
+def over_codes(codes, first, count, visit):
+    def step_code(step, code):
+        following = codes[first + step + 1, 0]
+        visit(code // 16, code % 16)
+        return following
+
+    lax.fori_loop(0, count, step_code, codes[first, 0])
+
 
 def group_kernel(
-    bodies, edges_hbm, tiles_ref, given_ref, acc_ref, features, weights, spread, points, edges, sem
+    bodies, codes, tiles_ref, given_ref, own_features, acc_ref, features, weights, spread, surface, points
 ):
     count, _, width = tiles_ref.shape
-    copy = pltpu.make_async_copy(edges_hbm, edges, sem)
-    copy.start()
+    rest = (count - 1) * width
+    pair_count = codes.shape[0] // 4
     for index in range(1, count):
+        tile = tiles_ref[index]
         columns = pl.ds((index - 1) * width, width)
-        prepare_tile(tiles_ref[index], bodies, columns, features, weights, spread)
+        for member in range(bodies):
+            features[member, columns, :] = source_features(*body_points(tile, bodies, member))
+            weights[member, :, columns] = body_weights(tile, member)
+        x, y, z, weight = surface_points(tile, bodies)
+        surface[columns, :] = source_features(x, y, z)
+        spread[columns, :] = jnp.broadcast_to(weight, (128, width)).T
     own = tiles_ref[0]
     for member in range(bodies):
         points[member] = rows_of((8, width), body_points(own, bodies, member))
-    acc_ref[...] = given_ref[...]
-    group_sums(bodies, edges, copy.wait, points, features, weights, spread, acc_ref)
+        features[member, rest:, :] = own_features[member]
+        weights[member, :, rest:] = body_weights(own, member)
+
+    def own_step(member, carry):
+        acc_ref[member] = given_ref[member] + influence_sum(
+            targets_of(points, member, 0.0), features[member, :rest, :], weights[member, :, :rest]
+        )
+        shift = (2 * member - (bodies - 1)).astype(full)
+        acc_ref[member, 0:1, :] += surface_sum(
+            targets_of(points, member, shift), surface[...], spread[...]
+        )
+        return carry
+
+    lax.fori_loop(0, bodies, own_step, 0)
+
+    def visit(target, source):
+        shift = (2 * (target - source)).astype(full)
+        acc_ref[target] += influence_sum(
+            targets_of(points, target, shift), features[source], weights[source]
+        )
+
+    over_codes(codes, 0, codes[4 * pair_count, 0], visit)
 
 
 def crossing_kernel(
-    bodies, edges_hbm, lower_ref, upper_ref, tile_ref, panels_ref, normals_ref, given_ref,
-    potential_hbm, force_ref, acc_ref, features, weights, points, edges, sems,
+    bodies, codes, lower_ref, upper_ref, tile_ref, panels_ref, normals_ref, given_ref,
+    acc_ref, force_ref, features, weights, points,
 ):
     count, _, width = lower_ref.shape
-    copy = pltpu.make_async_copy(edges_hbm, edges, sems.at[0])
-    copy.start()
+    pair_count = codes.shape[0] // 4
+    used = codes[4 * pair_count, 2]
+    crossings = codes[4 * pair_count, 1]
     own = tile_ref[...]
     for member in range(bodies):
         points[member] = rows_of((8, width), body_points(own, bodies, member))
     acc_ref[...] = given_ref[...]
     force_ref[...] = jnp.zeros_like(force_ref)
-    copy.wait()
     for slot in range(2 * bodies):
 
-        @pl.when(edges[4, 2 + slot] == 1)
+        @pl.when((jnp.right_shift(used, slot) & 1) == 1)
         def _():
             side = lower_ref if slot < bodies else upper_ref
             for index in range(count):
@@ -283,18 +303,14 @@
                 features[slot, columns, :] = source_features(*body_points(tile, bodies, member))
                 weights[slot, :, columns] = body_weights(tile, member)
 
-    def pair_step(step, carry):
-        target, source = edges[2, step], edges[3, step]
+    def visit(target, slot):
+        source = jnp.where(slot < bodies, slot - bodies, slot)
         shift = (2 * (target - source)).astype(full)
-        slot = jnp.where(source < 0, source + bodies, source)
         acc_ref[target] += influence_sum(
             targets_of(points, target, shift), features[slot], weights[slot]
         )
-        return carry
-
-    lax.fori_loop(0, edges[4, 1], pair_step, 0)
-    store = pltpu.make_async_copy(acc_ref, potential_hbm, sems.at[1])
-    store.start()
+
+    over_codes(codes, 2 * pair_count, crossings, visit)
     for member in range(bodies):
         area = panels_ref[3, member : member + 1, :]
         scaled = rows_of(
@@ -307,11 +323,15 @@
             precision=lax.Precision.HIGHEST,
             preferred_element_type=full,
         )
-    store.wait()
-
-
-def velocity_kernel(bodies, tiles_ref, features, given_ref, state_ref, next_ref, weights):
+
+
+def velocity_kernel(
+    bodies, tiles_ref, features, given_ref, state_ref, potential_ref, next_ref, potential_hbm, weights, sem
+):
     count, _, width = tiles_ref.shape
+    rest = (count - 1) * width
+    store = pltpu.make_async_copy(potential_ref, potential_hbm, sem)
+    store.start()
     for index in range(1, count):
         tile = tiles_ref[index]
         for member in range(bodies):
@@ -323,7 +343,7 @@
 
     def body_step(member, velocity):
         place = x + (bodies - 1 - 2 * member).astype(full)
-        term = velocity_term(features[member], weights[member], place, y, z)
+        term = velocity_term(features[member, :rest, :], weights[member], place, y, z)
         return tuple(so_far + part for so_far, part in zip(velocity, term))
 
     start = tuple(given_ref[axis : axis + 1, :] for axis in range(3))
@@ -332,9 +352,16 @@
     potential, elevation = state_ref[0:1, :], state_ref[1:2, :]
     next_ref[0:1, :] = potential + time_step * (-gravity * elevation - 0.5 * speed_sq)
     next_ref[1:2, :] = elevation + time_step * velocity[2]
-
-
-VMEM, SMEM, ANY = pltpu.VMEM, pltpu.SMEM, pl.ANY
+    store.wait()
+
+
+def finish_kernel(own_ref, first_ref, second_ref, third_ref, next_ref, force_ref, out_ref):
+    total = (own_ref[...] + second_ref[...]) + (first_ref[...] + third_ref[...])
+    force_ref[...] = total[:, :3, :8]
+    out_ref[...] = next_ref[...]
+
+
+VMEM, SMEM, HBM = pltpu.VMEM, pltpu.SMEM, pltpu.HBM
 
 
 def call(kernel, operands, results, scratch=(), units=0.0):
@@ -366,10 +393,11 @@
     width = body_panels.shape[2]
     tiles_count = lax.axis_size("surf")
     groups = lax.axis_size("body")
+    pair_count = pairs.shape[0]
     semaphore = pltpu.SemaphoreType.DMA
     own = call(
         pack_kernel,
-        [(ANY, body_panels), (ANY, fs_panels)],
+        [(HBM, body_panels), (HBM, fs_panels)],
         [(VMEM, (tile_rows(bodies), width), full)],
         scratch=(VMEM(body_panels.shape, full), VMEM(fs_panels.shape, full), semaphore((2,))),
     )
@@ -389,23 +417,21 @@
     wide = width * tiles_count
     rest = wide - width
     acc_shape = (bodies, 8, width)
-    edges_shape = (5, max(2 * pairs.shape[0], 2 + 2 * bodies))
     points = VMEM(acc_shape, full)
-    edges_space = SMEM(edges_shape, jnp.int32)
-    partial, velocity, edges = call(
+    partial, velocity, own_features, codes = call(
         functools.partial(own_tile_kernel, bodies),
-        [(ANY, pairs.T), (VMEM, own)],
+        [(HBM, pairs.T), (VMEM, own)],
         [
             (VMEM, acc_shape, full),
             (VMEM, (8, width), full),
-            (SMEM, edges_shape, jnp.int32),
+            (VMEM, (bodies + 1, width, DEPTH), half),
+            (VMEM, (code_rows(pair_count), 128), jnp.int32),
         ],
         scratch=(
-            VMEM((bodies + 1, width, DEPTH), half),
             VMEM((bodies, 16, width), half),
             VMEM((width, 128), full),
-            points,
-            SMEM((2, pairs.shape[0]), jnp.int32),
+            SMEM((2, pair_count), jnp.int32),
+            SMEM((3,), jnp.int32),
             semaphore,
         ),
         units=3.0,
@@ -414,45 +440,45 @@
     upper = lax.ppermute(tiles, "body", [(i + 1, i) for i in range(groups - 1)])
     partial, features = call(
         functools.partial(group_kernel, bodies),
-        [(ANY, edges), (VMEM, tiles), (VMEM, partial)],
-        [(VMEM, acc_shape, full), (VMEM, (bodies + 1, rest, DEPTH), half)],
+        [(VMEM, codes), (VMEM, tiles), (VMEM, partial), (VMEM, own_features)],
+        [(VMEM, acc_shape, full), (VMEM, (bodies, wide, DEPTH), half)],
         scratch=(
-            VMEM((bodies, 16, rest), half),
+            VMEM((bodies, 16, wide), half),
             VMEM((rest, 128), full),
+            VMEM((rest, DEPTH), half),
             points,
-            edges_space,
-            semaphore,
         ),
         units=7.0,
     )
-    own_potential, force = call(
+    potential, force = call(
         functools.partial(crossing_kernel, bodies),
-        [(ANY, edges), (VMEM, lower), (VMEM, upper), (VMEM, own), (VMEM, body_panels),
+        [(VMEM, codes), (VMEM, lower), (VMEM, upper), (VMEM, own), (VMEM, body_panels),
          (VMEM, body_normals), (VMEM, partial)],
-        [(ANY, acc_shape, full), (VMEM, (bodies, 8, 128), full)],
+        [(VMEM, acc_shape, full), (VMEM, (bodies, 8, 128), full)],
         scratch=(
-            VMEM(acc_shape, full),
             VMEM((2 * bodies, wide, DEPTH), half),
             VMEM((2 * bodies, 16, wide), half),
             points,
-            edges_space,
-            semaphore((2,)),
         ),
         units=6.0,
     )
-    fs_next = call(
+    fs_next, own_potential = call(
         functools.partial(velocity_kernel, bodies),
-        [(VMEM, tiles), (VMEM, features), (VMEM, velocity), (VMEM, fs_state)],
-        [(VMEM, (2, width), full)],
-        scratch=(VMEM((bodies, 16, rest), half),),
+        [(VMEM, tiles), (VMEM, features), (VMEM, velocity), (VMEM, fs_state), (VMEM, potential)],
+        [(VMEM, (2, width), full), (HBM, acc_shape, full)],
+        scratch=(VMEM((bodies, 16, rest), half), semaphore),
         units=5.0,
     )
     if tiles_count == 4:
-        first, second, third = rotations(force, "surf")
-        total = (force + second) + (first + third)
+        pieces = [force] + rotations(force, "surf")
     else:
-        total = lax.psum(force, "surf")
-    return own_potential, total[:, :3, :8].transpose(0, 2, 1), fs_next
+        pieces = [lax.psum(force, "surf")] + [jnp.zeros_like(force)] * 3
+    total, fs_next = call(
+        finish_kernel,
+        [(VMEM, piece) for piece in pieces] + [(VMEM, fs_next)],
+        [(VMEM, (bodies, 3, 8), full), (VMEM, (2, width), full)],
+    )
+    return own_potential, total.transpose(0, 2, 1), fs_next
 
 
 def solution(mesh):

time: 45.1 us -> 43.6 us (0.967)
  the two profiles are of different devices: /device:TPU:2 before, /device:TPU:5 now
where the time goes in v3:
time: 43.6 us; the launch traced here: 44 us
  Pallas kernels  24.4 us (56%)
  starting transfers between devices  13.8 us (32%)
  waiting for transfers between devices  2.73 us (6%)
  local copies, waits for them, and re-layouts  2.28 us (5%)
  between operations  0.77 us (2%)
    pallas_call x6, Pallas kernels, call(): pl.pallas_call(kernel, out_shape=[jax.ShapeDtypeStruct(shape, kind) for _...  24.4 us
    ppermute x6, starting transfers between devices, rotations(): lax.ppermute(block, axis, [(i, (i + k) % count) for i in range(count)])  8.03 us
    ppermute x1, starting transfers between devices, on_device(): lower = lax.ppermute(tiles, 'body', [(i, i + 1) for i in range(groups - 1)])  3.81 us
    ppermute x6, waiting for transfers between devices, rotations(): lax.ppermute(block, axis, [(i, (i + k) % count) for i in range(count)])  2.73 us
    unnamed x12, local copies, waits for them, and re-layouts  2.28 us
    ppermute x1, starting transfers between devices, on_device(): upper = lax.ppermute(tiles, 'body', [(i + 1, i) for i in range(groups - 1)])  1.92 us
  transfers between devices with their start and end apart: 8, of which 1 were waited for; matrix products, arithmetic and copies ran while one was open for 0% of the time, Pallas kernels for 44%

profile of v3, /device:TPU:5, one launch (start us, length us, event | category | flops | bytes accessed | tf_op | source)
XLA Modules:
  0.0 44.0 jit_solution(16491477841254242340)
XLA Ops:
  0.6 0.0 copy-start
  0.6 0.9 %copy-done = f32[12,3,512]{2,1,0:T(4,128)S(1)} copy-done((f32[12,3,512]{2,1,0:T(4,128)S(1)}, f32[12,3,512]{2,1,0:T(4,128)}, u32[]{:S(2)}) %copy-start) | copy-done | bytes 73752
  1.5 0.0 copy-start.2
  1.5 0.7 %copy-done.2 = f32[4,512]{1,0:T(4,128)S(1)} copy-done((f32[4,512]{1,0:T(4,128)S(1)}, f32[4,512]{1,0:T(4,128)}, u32[]{:S(2)}) %copy-start.2) | copy-done | bytes 8216
  2.2 0.2 shard_map.76.tile_ref
  2.4 3.4 %collective-permute-start.2 = (f32[40,512]{1,0:T(8,128)S(1)}, f32[40,512]{1,0:T(8,128)S(1)}, u32[]{:S(2)}, u32[]{:S(2)}) collective-permute-start(f32[40,512]{1,0:T(8,128)S(1)} %shard_map.76.tile_ref), channel_id=1, source_target_pairs={{0,3},{1,0},{2,1},{3,2},{4,7},{5,4},{6,5},{7,6},{8,11},{9,8},{10,9... | collective-permute-start | bytes 245768 | tf_op jit(solution)/shard_map/ppermute | solution.py:386
  5.8 0.0 collective-permute-start.1
  5.8 0.5 %collective-permute-start = (f32[40,512]{1,0:T(8,128)S(1)}, f32[40,512]{1,0:T(8,128)S(1)}, u32[]{:S(2)}, u32[]{:S(2)}) collective-permute-start(f32[40,512]{1,0:T(8,128)S(1)} %shard_map.76.tile_ref), channel_id=1, source_target_pairs={{0,1},{1,2},{2,3},{3,0},{4,5},{5,6},{6,7},{7,4},{8,9},{9,10},{10,1... | collective-permute-start | bytes 245768 | tf_op jit(solution)/shard_map/ppermute | solution.py:386
  6.2 0.0 copy-start.5
  6.2 0.7 %copy-done.5 = s32[18,2]{0,1:T(2,128)S(1)} copy-done((s32[18,2]{0,1:T(2,128)S(1)}, s32[18,2]{0,1:T(2,128)}, u32[]{:S(2)}) %copy-start.5) | copy-done | bytes 168
  6.9 3.8 %shard_map.77 = (f32[3,8,512]{2,1,0:T(8,128)S(1)}, f32[8,512]{1,0:T(8,128)S(1)}, bf16[4,512,48]{2,1,0:T(8,128)(2,1)S(1)}, s32[73,128]{1,0:T(8,128)S(1)}) custom-call(s32[2,18]{1,0:T(2,128)S(1)} %bitcast.7, f32[40,512]{1,0:T(8,128)S(1)} %shard_map.76.tile_ref), custom_call_target="tpu_custom_call" | custom-call | flops 3600000000 | bytes 1024 | tf_op jit(solution)/shard_map/pallas_call | solution.py:369
  10.7 0.0 collective-permute-done.2
  10.7 2.7 %collective-permute-done.1 = f32[40,512]{1,0:T(8,128)S(1)} collective-permute-done((f32[40,512]{1,0:T(8,128)S(1)}, f32[40,512]{1,0:T(8,128)S(1)}, u32[]{:S(2)}, u32[]{:S(2)}) %collective-permute-start.1) | collective-permute-done | bytes 81952 | tf_op jit(solution)/shard_map/ppermute | solution.py:386
  13.4 0.0 collective-permute-done
  13.5 3.8 %collective-permute-start.3 = (f32[4,40,512]{2,1,0:T(8,128)S(1)}, f32[4,40,512]{2,1,0:T(8,128)S(1)}, u32[]{:S(2)}, u32[]{:S(2)}) collective-permute-start(f32[4,40,512]{2,1,0:T(8,128)S(1)} %pad_maximum_fusion.tiles_ref), channel_id=1, source_target_pairs={{0,4},{4,8},{8,12},{12,16},{16,20},{20,24},{24,28},{1,5},{5,9},{9,... | collective-permute-start | bytes 983048 | tf_op jit(solution)/shard_map/ppermute | solution.py:439
  17.3 1.9 %collective-permute-start.4 = (f32[4,40,512]{2,1,0:T(8,128)S(1)}, f32[4,40,512]{2,1,0:T(8,128)S(1)}, u32[]{:S(2)}, u32[]{:S(2)}) collective-permute-start(f32[4,40,512]{2,1,0:T(8,128)S(1)} %pad_maximum_fusion.tiles_ref), channel_id=1, source_target_pairs={{4,0},{8,4},{12,8},{16,12},{20,16},{24,20},{28,24},{5,1},{9,5},{13... | collective-permute-start | bytes 983048 | tf_op jit(solution)/shard_map/ppermute | solution.py:440
  19.2 0.0 copy-start.1
  19.2 0.0 copy-start.3
  19.2 12.1 %shard_map.78 = (f32[3,8,512]{2,1,0:T(8,128)S(1)}, bf16[3,2048,48]{2,1,0:T(8,128)(2,1)S(1)}) custom-call(s32[73,128]{1,0:T(8,128)S(1)} %get-tuple-element.15.codes, f32[4,40,512]{2,1,0:T(8,128)S(1)} %pad_maximum_fusion.tiles_ref, f32[3,8,512]{2,1,0:T(8,128)S(1)} %get-tuple-element.16.given_ref, bf16[4,512,48]{2,1,0:T(8,128)(2,1)S(1)} %get-tuple-element.17.own_features), custom_call_target="tpu_custom_call" | custom-call | flops 8400000000 | bytes 1024 | tf_op jit(solution)/shard_map/pallas_call | solution.py:369
  31.4 0.0 collective-permute-done.3.lower_ref
  31.4 0.0 collective-permute-done.4.upper_ref
  31.4 0.0 copy-done.1
  31.4 0.0 copy-done.3
  31.4 0.0 copy-start.4
  31.4 4.4 %shard_map.79 = (f32[3,8,512]{2,1,0:T(8,128)S(1)}, f32[3,8,128]{2,1,0:T(8,128)S(1)}) custom-call(s32[73,128]{1,0:T(8,128)S(1)} %get-tuple-element.15.codes, f32[4,40,512]{2,1,0:T(8,128)S(1)} %collective-permute-done.3.lower_ref, f32[4,40,512]{2,1,0:T(8,128)S(1)} %collective-permute-done.4.upper_ref, f32[40,512]{1,0:T(8,128)S(1)} %shard_map.76.tile_ref, ...), custom_call_target="tpu_custom_call" | custom-call | flops 7200000000 | bytes 1024 | tf_op jit(solution)/shard_map/pallas_call | solution.py:369
  35.8 0.2 collective-permute-start.5
  36.0 1.9 %collective-permute-start.6 = (f32[3,8,128]{2,1,0:T(8,128)S(1)}, f32[3,8,128]{2,1,0:T(8,128)S(1)}, u32[]{:S(2)}, u32[]{:S(2)}) collective-permute-start(f32[3,8,128]{2,1,0:T(8,128)S(1)} %get-tuple-element.23.own_ref), channel_id=1, source_target_pairs={{0,2},{1,3},{2,0},{3,1},{4,6},{5,7},{6,4},{7,5},{8,10},{9,11},{10,... | collective-permute-start | bytes 36872 | tf_op jit(solution)/shard_map/ppermute | solution.py:386
  38.0 2.1 %collective-permute-start.7 = (f32[3,8,128]{2,1,0:T(8,128)S(1)}, f32[3,8,128]{2,1,0:T(8,128)S(1)}, u32[]{:S(2)}, u32[]{:S(2)}) collective-permute-start(f32[3,8,128]{2,1,0:T(8,128)S(1)} %get-tuple-element.23.own_ref), channel_id=1, source_target_pairs={{0,3},{1,0},{2,1},{3,2},{4,7},{5,4},{6,5},{7,6},{8,11},{9,8},{10,9... | collective-permute-start | bytes 36872 | tf_op jit(solution)/shard_map/ppermute | solution.py:386
  40.0 0.0 copy-done.4
  40.0 3.3 %shard_map.80 = (f32[2,512]{1,0:T(2,128)S(1)}, f32[3,8,512]{2,1,0:T(8,128)}) custom-call(f32[4,40,512]{2,1,0:T(8,128)S(1)} %pad_maximum_fusion.tiles_ref, bf16[3,2048,48]{2,1,0:T(8,128)(2,1)S(1)} %get-tuple-element.18.features, f32[8,512]{1,0:T(8,128)S(1)} %get-tuple-element.19.given_ref, f32[2,512]{1,0:T(2,128)S(1)} %copy-done.4, ...), custom_call_target="tpu_custom_call" | custom-call | flops 6000000000 | bytes 1024 | tf_op jit(solution)/shard_map/pallas_call | solution.py:369
  43.3 0.0 collective-permute-done.5.first_ref
  43.4 0.0 collective-permute-done.6.second_ref
  43.4 0.0 collective-permute-done.7.third_ref
  43.4 0.6 %shard_map.81 = (f32[3,3,8]{2,1,0:T(4,128)}, f32[2,512]{1,0:T(2,128)}) custom-call(f32[3,8,128]{2,1,0:T(8,128)S(1)} %get-tuple-element.23.own_ref, f32[3,8,128]{2,1,0:T(8,128)S(1)} %collective-permute-done.5.first_ref, f32[3,8,128]{2,1,0:T(8,128)S(1)} %collective-permute-done.6.second_ref, f32[3,8,128]{2,1,0:T(8,128)S(1)} %collective-permute-done.7.third_ref, ...), custom_call_target="tpu_custom_call" | custom-call | bytes 1024 | tf_op jit(solution)/shard_map/pallas_call | solution.py:369
  (1 shorter events, 0.0 us)
Async XLA Ops:
  0.6 0.9 %copy-start = (f32[12,3,512]{2,1,0:T(4,128)S(1)}, f32[12,3,512]{2,1,0:T(4,128)}, u32[]{:S(2)}) copy-start(f32[12,3,512]{2,1,0:T(4,128)} %panels_ref.1) | copy-start | bytes 221188
  1.5 0.7 %copy-start.2 = (f32[4,512]{1,0:T(4,128)S(1)}, f32[4,512]{1,0:T(4,128)}, u32[]{:S(2)}) copy-start(f32[4,512]{1,0:T(4,128)} %surface_hbm.1) | copy-start | bytes 24580
  2.4 8.3 %collective-permute-start.2 = (f32[40,512]{1,0:T(8,128)S(1)}, f32[40,512]{1,0:T(8,128)S(1)}, u32[]{:S(2)}, u32[]{:S(2)}) collective-permute-start(f32[40,512]{1,0:T(8,128)S(1)} %shard_map.76.tile_ref), channel_id=1, source_target_pairs={{0,3},{1,0},{2,1},{3,2},{4,7},{5,4},{6,5},{7,6},{8,11},{9,8},{10,9... | collective-permute-start | bytes 245768 | tf_op jit(solution)/shard_map/ppermute | solution.py:386
  5.8 7.7 %collective-permute-start.1 = (f32[40,512]{1,0:T(8,128)S(1)}, f32[40,512]{1,0:T(8,128)S(1)}, u32[]{:S(2)}, u32[]{:S(2)}) collective-permute-start(f32[40,512]{1,0:T(8,128)S(1)} %shard_map.76.tile_ref), channel_id=1, source_target_pairs={{0,2},{1,3},{2,0},{3,1},{4,6},{5,7},{6,4},{7,5},{8,10},{9,11},{10,... | collective-permute-start | bytes 245768 | tf_op jit(solution)/shard_map/ppermute | solution.py:386
  5.8 7.7 %collective-permute-start = (f32[40,512]{1,0:T(8,128)S(1)}, f32[40,512]{1,0:T(8,128)S(1)}, u32[]{:S(2)}, u32[]{:S(2)}) collective-permute-start(f32[40,512]{1,0:T(8,128)S(1)} %shard_map.76.tile_ref), channel_id=1, source_target_pairs={{0,1},{1,2},{2,3},{3,0},{4,5},{5,6},{6,7},{7,4},{8,9},{9,10},{10,1... | collective-permute-start | bytes 245768 | tf_op jit(solution)/shard_map/ppermute | solution.py:386
  6.2 0.7 %copy-start.5 = (s32[18,2]{0,1:T(2,128)S(1)}, s32[18,2]{0,1:T(2,128)}, u32[]{:S(2)}) copy-start(s32[18,2]{0,1:T(2,128)} %param.9) | copy-start | bytes 436
  13.5 17.9 %collective-permute-start.3 = (f32[4,40,512]{2,1,0:T(8,128)S(1)}, f32[4,40,512]{2,1,0:T(8,128)S(1)}, u32[]{:S(2)}, u32[]{:S(2)}) collective-permute-start(f32[4,40,512]{2,1,0:T(8,128)S(1)} %pad_maximum_fusion.tiles_ref), channel_id=1, source_target_pairs={{0,4},{4,8},{8,12},{12,16},{16,20},{20,24},{24,28},{1,5},{5,9},{9,... | collective-permute-start | bytes 983048 | tf_op jit(solution)/shard_map/ppermute | solution.py:439
  17.3 14.1 %collective-permute-start.4 = (f32[4,40,512]{2,1,0:T(8,128)S(1)}, f32[4,40,512]{2,1,0:T(8,128)S(1)}, u32[]{:S(2)}, u32[]{:S(2)}) collective-permute-start(f32[4,40,512]{2,1,0:T(8,128)S(1)} %pad_maximum_fusion.tiles_ref), channel_id=1, source_target_pairs={{4,0},{8,4},{12,8},{16,12},{20,16},{24,20},{28,24},{5,1},{9,5},{13... | collective-permute-start | bytes 983048 | tf_op jit(solution)/shard_map/ppermute | solution.py:440
  19.2 12.2 %copy-start.1 = (f32[12,3,512]{2,1,0:T(4,128)S(1)}, f32[12,3,512]{2,1,0:T(4,128)}, u32[]{:S(2)}) copy-start(f32[12,3,512]{2,1,0:T(4,128)} %panels_ref.1) | copy-start | bytes 221188
  19.2 12.2 %copy-start.3 = (f32[3,3,512]{2,1,0:T(4,128)S(1)}, f32[3,3,512]{2,1,0:T(4,128)}, u32[]{:S(2)}) copy-start(f32[3,3,512]{2,1,0:T(4,128)} %normals_ref.1) | copy-start | bytes 55300
  31.4 8.6 %copy-start.4 = (f32[2,512]{1,0:T(2,128)S(1)}, f32[2,512]{1,0:T(2,128)}, u32[]{:S(2)}) copy-start(f32[2,512]{1,0:T(2,128)} %state_ref.1) | copy-start | bytes 12292
  35.8 7.5 %collective-permute-start.5 = (f32[3,8,128]{2,1,0:T(8,128)S(1)}, f32[3,8,128]{2,1,0:T(8,128)S(1)}, u32[]{:S(2)}, u32[]{:S(2)}) collective-permute-start(f32[3,8,128]{2,1,0:T(8,128)S(1)} %get-tuple-element.23.own_ref), channel_id=1, source_target_pairs={{0,1},{1,2},{2,3},{3,0},{4,5},{5,6},{6,7},{7,4},{8,9},{9,10},{10,1... | collective-permute-start | bytes 36872 | tf_op jit(solution)/shard_map/ppermute | solution.py:386
  36.0 7.3 %collective-permute-start.6 = (f32[3,8,128]{2,1,0:T(8,128)S(1)}, f32[3,8,128]{2,1,0:T(8,128)S(1)}, u32[]{:S(2)}, u32[]{:S(2)}) collective-permute-start(f32[3,8,128]{2,1,0:T(8,128)S(1)} %get-tuple-element.23.own_ref), channel_id=1, source_target_pairs={{0,2},{1,3},{2,0},{3,1},{4,6},{5,7},{6,4},{7,5},{8,10},{9,11},{10,... | collective-permute-start | bytes 36872 | tf_op jit(solution)/shard_map/ppermute | solution.py:386
  38.0 5.4 %collective-permute-start.7 = (f32[3,8,128]{2,1,0:T(8,128)S(1)}, f32[3,8,128]{2,1,0:T(8,128)S(1)}, u32[]{:S(2)}, u32[]{:S(2)}) collective-permute-start(f32[3,8,128]{2,1,0:T(8,128)S(1)} %get-tuple-element.23.own_ref), channel_id=1, source_target_pairs={{0,3},{1,0},{2,1},{3,2},{4,7},{5,4},{6,5},{7,6},{8,11},{9,8},{10,9... | collective-permute-start | bytes 36872 | tf_op jit(solution)/shard_map/ppermute | solution.py:386
